TPU v7x, 512 devices: a whole 4x4x16 slice. The times are simulated.
512 devices in a mesh: ctx: 128 (over z, y, x_hi), head: 4 (over x_lo, core).
Axes of the slice: x: 4 (x_hi: 2, x_lo: 2; x = x_hi * 2 + x_lo), y: 4, z: 16, core: 2. Of those that a mesh axis runs over, the one named last changes fastest.
Arguments:
- query_rows: bfloat16 [2, 8192, 3072], P(None, 'ctx', 'head'), may hold values from -4 to 4
- key_rows: bfloat16 [2, 8192, 3072], P(None, 'ctx', 'head'), may hold values from -4 to 4
- value_rows: bfloat16 [2, 8192, 3072], P(None, 'ctx', 'head'), may hold values from -4 to 4
- out_grad: bfloat16 [2, 8192, 3072], P(None, 'ctx', 'head'), may hold values from -16 to 16
- log_norms: float32 [2, 2, 12, 8192], P(None, None, 'head', 'ctx'), may hold values from 3 to 4.5
- row_deltas: float32 [2, 2, 12, 8192], P(None, None, 'head', 'ctx'), may hold values from -16 to 16
- lambdas: float32 [12], P('head'), may hold values from 0.3 to 0.9
Outputs:
- query_grad: bfloat16 [2, 8192, 3072], P(None, ('ctx', 'head'))
- key_grad: bfloat16 [2, 8192, 3072], P(None, ('ctx', 'head'))
- value_grad: bfloat16 [2, 8192, 3072], P(None, ('ctx', 'head'))
- lambda_grad: float32 [12], P('head')
All inputs are finite; a program needn't handle non-finite values.
Results may differ from a plain program's by a relative error of at most 0.039.
Values may be sent and summed in bfloat16 or wider, within the bound.
A program may use at most 64 MiB of HBM per device.

v0:
```python
import math

import jax
import jax.numpy as jnp
from jax import lax
from jax.sharding import PartitionSpec as P

CYCLE = 3


def passed_along(shard, axis, by):
    peers = lax.axis_size(axis)
    return lax.ppermute(shard, axis, [(i, (i + by) % peers) for i in range(peers)])


def shortened(shard):
    return jax.tree.map(lambda a: a.astype(jnp.bfloat16) if a.dtype == jnp.float32 else a, shard)


def tile_grads(
    query_tile, key_tile, value_tile, grad_tile, norm_tile, delta_tile, lambdas, allowed
):
    single = jnp.float32
    score_scale = 1.0 / math.sqrt(query_tile.shape[-1])
    scores = (
        jnp.einsum("qhmc,khmc->hmqk", query_tile, key_tile, preferred_element_type=single)
        * score_scale
    )
    attn_probs = jnp.where(
        allowed[None, None], jnp.exp(scores - jnp.swapaxes(norm_tile, 0, 1)[:, :, :, None]), 0.0
    )
    grad_inner = jnp.einsum("qhc,khc->hqk", grad_tile, value_tile, preferred_element_type=single)
    mixed_probs = (attn_probs[:, 0] - lambdas[:, None, None] * attn_probs[:, 1]).astype(
        jnp.bfloat16
    )
    value_grad = jnp.einsum("hqk,qhc->khc", mixed_probs, grad_tile, preferred_element_type=single)
    factor = jnp.stack([jnp.ones_like(lambdas), -lambdas], axis=1)[:, :, None, None]
    shifted = grad_inner[:, None] - jnp.swapaxes(delta_tile, 0, 1)[:, :, :, None]
    score_grad = (score_scale * factor * attn_probs * shifted).astype(jnp.bfloat16)
    query_grad = jnp.einsum("hmqk,khmc->qhmc", score_grad, key_tile, preferred_element_type=single)
    key_grad = jnp.einsum("hmqk,qhmc->khmc", score_grad, query_tile, preferred_element_type=single)
    lambda_part = -jnp.sum(attn_probs[:, 1] * grad_inner, axis=(1, 2))
    return (query_grad, key_grad, value_grad, lambda_part)


def positions(half_index, owner, block_rows, seq_len):
    start = jnp.where(half_index == 0, owner * block_rows, seq_len - block_rows * (owner + 1))
    return start + jnp.arange(block_rows, dtype=jnp.int32)


def select_half(stacked, half_index):
    return stacked[half_index]


def add_half(totals, half_index, term):
    totals[half_index] = totals[half_index] + term


def step_terms(q_owner, k_owner, query_pack, key_pack, lambdas, block_count):
    query_five, grad_four, norm_four, delta_four = query_pack
    key_five, value_four = key_pack
    block_rows = query_five.shape[1]
    seq_len = 2 * block_count * block_rows
    pairs = [(0, 0), (0, 1), (1, 0), (1, 1)]
    query_parts = [
        jnp.zeros(query_five.shape[1:], jnp.float32),
        jnp.zeros(query_five.shape[1:], jnp.float32),
    ]
    key_parts = [
        jnp.zeros(key_five.shape[1:], jnp.float32),
        jnp.zeros(key_five.shape[1:], jnp.float32),
    ]
    value_parts = [
        jnp.zeros(value_four.shape[1:], jnp.float32),
        jnp.zeros(value_four.shape[1:], jnp.float32),
    ]
    lambda_total = jnp.zeros(lambdas.shape, jnp.float32)
    for query_half, key_half in pairs:
        allowed = (
            positions(key_half, k_owner, block_rows, seq_len)[None, :]
            <= positions(query_half, q_owner, block_rows, seq_len)[:, None]
        )
        tile_terms = tile_grads(
            select_half(query_five, query_half),
            select_half(key_five, key_half),
            select_half(value_four, key_half),
            select_half(grad_four, query_half),
            select_half(norm_four, query_half),
            select_half(delta_four, query_half),
            lambdas,
            allowed,
        )
        add_half(query_parts, query_half, tile_terms[0])
        add_half(key_parts, key_half, tile_terms[1])
        add_half(value_parts, key_half, tile_terms[2])
        lambda_total = lambda_total + tile_terms[3]
    return (jnp.stack(query_parts), jnp.stack(key_parts), jnp.stack(value_parts), lambda_total)


def local(query_rows, key_rows, value_rows, out_grad, log_norms, row_deltas, lambdas):
    block_count = lax.axis_size("ctx")
    own_index = lax.axis_index("ctx")
    block_rows = query_rows.shape[1]
    heads_here = lambdas.shape[0]
    query_five = query_rows.reshape(2, block_rows, heads_here, 2, -1)
    key_five = key_rows.reshape(2, block_rows, heads_here, 2, -1)
    value_four = value_rows.reshape(2, block_rows, heads_here, -1)
    grad_four = out_grad.reshape(2, block_rows, heads_here, -1)
    query_pack = (query_five, grad_four, log_norms, row_deltas)
    key_pack = (key_five, value_four)
    lambda_total = jnp.zeros((heads_here,), jnp.float32)
    query_total = jnp.zeros(query_five.shape, jnp.float32)
    pair_steps = []
    for visit_step in range(CYCLE):
        if visit_step > 0:
            key_pack = passed_along((key_pack[0], key_pack[1]), "ctx", -1)
        k_owner = (own_index + visit_step) % block_count
        step_query, step_key, step_value, step_lambda = step_terms(
            own_index, k_owner, query_pack, key_pack, lambdas, block_count
        )
        query_total = query_total + step_query
        pair_steps.append((step_key, step_value))
        lambda_total = lambda_total + step_lambda
    back_pair = pair_steps[CYCLE - 1]
    for visit_step in range(CYCLE - 2, -1, -1):
        moved = passed_along((shortened(back_pair[0]), shortened(back_pair[1])), "ctx", 1)
        back_pair = (moved[0] + pair_steps[visit_step][0], moved[1] + pair_steps[visit_step][1])
    key_total, value_total = back_pair
    query_out = query_total.reshape(2, block_rows, -1).astype(jnp.bfloat16)
    key_out = key_total.reshape(2, block_rows, -1).astype(jnp.bfloat16)
    value_out = value_total.reshape(2, block_rows, -1).astype(jnp.bfloat16)
    query_out, key_out, value_out = (
        lax.all_to_all(query_out, "head", split_axis=1, concat_axis=2, tiled=True),
        lax.all_to_all(key_out, "head", split_axis=1, concat_axis=2, tiled=True),
        lax.all_to_all(value_out, "head", split_axis=1, concat_axis=2, tiled=True),
    )
    lambda_grad = lax.psum(lambda_total, "ctx")
    return (query_out, key_out, value_out, lambda_grad)


def solution(mesh):
    in_specs = (
        P(None, "ctx", "head"),
        P(None, "ctx", "head"),
        P(None, "ctx", "head"),
        P(None, "ctx", "head"),
        P(None, None, "head", "ctx"),
        P(None, None, "head", "ctx"),
        P("head"),
    )
    out_specs = (
        P(None, ("ctx", "head"), None),
        P(None, ("ctx", "head"), None),
        P(None, ("ctx", "head"), None),
        P("head"),
    )
    return jax.shard_map(local, mesh=mesh, in_specs=in_specs, out_specs=out_specs, check_vma=False)
```

profile of v0, /device:TPU:6, one launch (start us, length us, event | category | flops | bytes accessed | tf_op | source)
XLA Modules:
  0.0 463.6 jit_solution(3893372137987177488)
XLA Ops:
  0.6 1.0 reshape.424
  1.7 3.4 collective-permute-start
  5.2 15.5 %collective-permute-start.1 = (bf16[2,64,3,256]{3,1,2,0:T(8,128)(2,1)S(1)}, bf16[2,64,3,256]{3,1,2,0:T(8,128)(2,1)S(1)}, u32[]{:S(2)}, u32[]{:S(2)}) collective-permute-start(bf16[2,64,3,256]{3,1,2,0:T(8,128)(2,1)S(1)} %bitcast.343), channel_id=1, source_target_pairs={{0,508},{4,0},{8,4},{12,8},{16,12},{20,16},{24,20},{28,24},{32,28}... | collective-permute-start | bytes 589832 | tf_op jit(solution)/shard_map/ppermute | solution.py:13
  20.8 0.9 copy-done.9
  22.9 0.6 copy-done.13
  23.6 0.6 copy-done.11
  25.0 0.8 multiply_reduce_fusion.10
  26.5 0.8 multiply_reduce_fusion.8
  27.6 0.8 multiply_reduce_fusion.9
  28.4 0.7 multiply_reduce_fusion.11
  30.6 3.3 collective-permute-start.2
  34.2 1.0 fusion.47
  35.2 4.2 collective-permute-start.3
  39.4 0.8 multiply_reduce_fusion.4
  40.2 0.8 multiply_reduce_fusion.5
  41.0 0.8 multiply_reduce_fusion.6
  41.9 0.7 multiply_reduce_fusion.7
  43.6 1.7 collective-permute-done.3
  45.3 0.8 multiply_reduce_fusion.2
  46.1 0.8 multiply_reduce_fusion.3
  48.1 0.8 multiply_reduce_fusion
  49.6 0.7 pad_maximum_fusion.1
  50.3 4.0 collective-permute-start.6
  54.6 1.0 fusion.48
  56.5 0.7 pad_maximum_fusion
  57.2 2.4 collective-permute-start.4
  60.2 0.9 fusion.1
  61.9 0.8 stack.123
  63.2 0.8 stack.124
  64.5 0.8 stack.120
  65.3 0.9 fusion.3
  69.1 0.9 copy.397
  69.9 4.2 all-to-all-start
  74.5 0.7 copy-done.2
  75.2 1.0 fusion.62
  76.1 2.7 collective-permute-start.7
  78.8 1.0 fusion.60
  79.8 1.9 collective-permute-start.5
  81.7 5.8 %collective-permute-done.7 = bf16[2,64,3,256]{3,1,2,0:T(8,128)(2,1)S(1)} collective-permute-done((bf16[2,64,3,256]{3,1,2,0:T(8,128)(2,1)S(1)}, bf16[2,64,3,256]{3,1,2,0:T(8,128)(2,1)S(1)}, u32[]{:S(2)}, u32[]{:S(2)}) %collective-permute-start.7) | collective-permute-done | bytes 196640 | tf_op jit(solution)/shard_map/ppermute | solution.py:13
  87.7 0.8 reshape.427
  88.6 3.5 all-to-all-start.2
  92.4 0.8 reshape.426
  93.1 2.6 all-to-all-done.2
  95.7 5.0 %all-to-all-start.1 = ((bf16[2,64,768]{2,0,1:T(2,128)(2,1)}), bf16[2,64,768]{2,0,1:T(2,128)(2,1)S(1)}, u32[]{:S(2)}, u32[]{:S(2)}) async-start(bf16[2,64,768]{2,0,1:T(2,128)(2,1)} %reshape.426), calls=%async_computation.1 | async-start | bytes 393216 | tf_op jit(solution)/shard_map/all_to_all | solution.py:134
  101.5 360.0 %psum.7 = f32[3]{0:T(128)} all-reduce(f32[3]{0:T(128)S(1)} %add_add_fusion), channel_id=1, replica_groups=mesh['ctx'=128,'head'=4] {'ctx'}, use_global_device_ids=true, to_apply=%region_12.13 | all-reduce | flops 3 | bytes 24 | tf_op jit(solution)/shard_map/psum | solution.py:137
  461.5 0.7 copy.554
  462.2 0.7 copy.556
  462.9 0.7 copy.555
  (150 shorter events, 15.1 us)
Async XLA Ops:
  1.6 3.5 copy-start.1
  1.7 27.5 %collective-permute-start = (bf16[2,64,3,2,128]{4,1,3,2,0:T(8,128)(2,1)S(1)}, bf16[2,64,3,2,128]{4,1,3,2,0:T(8,128)(2,1)S(1)}, u32[]{:S(2)}, u32[]{:S(2)}) collective-permute-start(bf16[2,64,3,2,128]{4,1,3,2,0:T(8,128)(2,1)S(1)} %copy.359), channel_id=1, source_target_pairs={{0,508},{4,0},{8,4},{12,8},{16,12},{20,16},{24,20},{28,24},{32,28}... | collective-permute-start | bytes 589832 | tf_op jit(solution)/shard_map/ppermute | solution.py:13
  5.1 15.6 %copy-start = (bf16[2,64,768]{2,1,0:T(8,128)(2,1)S(1)}, bf16[2,64,768]{2,1,0:T(8,128)(2,1)}, u32[]{:S(2)}) copy-start(bf16[2,64,768]{2,1,0:T(8,128)(2,1)} %param.8) | copy-start | bytes 589828
  5.2 30.1 %collective-permute-start.1 = (bf16[2,64,3,256]{3,1,2,0:T(8,128)(2,1)S(1)}, bf16[2,64,3,256]{3,1,2,0:T(8,128)(2,1)S(1)}, u32[]{:S(2)}, u32[]{:S(2)}) collective-permute-start(bf16[2,64,3,256]{3,1,2,0:T(8,128)(2,1)S(1)} %bitcast.343), channel_id=1, source_target_pairs={{0,508},{4,0},{8,4},{12,8},{16,12},{20,16},{24,20},{28,24},{32,28}... | collective-permute-start | bytes 589832 | tf_op jit(solution)/shard_map/ppermute | solution.py:13
  20.8 0.9 copy-start.9
  21.7 0.7 copy-start.12
  21.7 0.9 copy-start.10
  22.9 0.7 copy-start.13
  23.6 0.7 copy-start.11
  30.6 12.0 %collective-permute-start.2 = (bf16[2,64,3,2,128]{4,1,3,2,0:T(8,128)(2,1)S(1)}, bf16[2,64,3,2,128]{4,1,3,2,0:T(8,128)(2,1)S(1)}, u32[]{:S(2)}, u32[]{:S(2)}) collective-permute-start(bf16[2,64,3,2,128]{4,1,3,2,0:T(8,128)(2,1)S(1)} %collective-permute-done), channel_id=1, source_target_pairs={{0,508},{4,0},{8,4},{12,8},{16,12},{20,16},{24,20},{28,24},{32,28}... | collective-permute-start | bytes 589832 | tf_op jit(solution)/shard_map/ppermute | solution.py:13
  35.2 10.1 %collective-permute-start.3 = (bf16[2,64,3,256]{3,1,2,0:T(8,128)(2,1)S(1)}, bf16[2,64,3,256]{3,1,2,0:T(8,128)(2,1)S(1)}, u32[]{:S(2)}, u32[]{:S(2)}) collective-permute-start(bf16[2,64,3,256]{3,1,2,0:T(8,128)(2,1)S(1)} %collective-permute-done.1), channel_id=1, source_target_pairs={{0,508},{4,0},{8,4},{12,8},{16,12},{20,16},{24,20},{28,24},{32,28}... | collective-permute-start | bytes 589832 | tf_op jit(solution)/shard_map/ppermute | solution.py:13
  50.3 24.1 %collective-permute-start.6 = (bf16[2,64,3,256]{3,1,2,0:T(8,128)(2,1)}, bf16[2,64,3,256]{3,1,2,0:T(8,128)(2,1)}, u32[]{:S(2)}, u32[]{:S(2)}) collective-permute-start(bf16[2,64,3,256]{3,1,2,0:T(8,128)(2,1)} %pad_maximum_fusion.1), channel_id=1, source_target_pairs={{0,4},{4,8},{8,12},{12,16},{16,20},{20,24},{24,28},{28,32},{32,36}... | collective-permute-start | bytes 589832 | tf_op jit(solution)/shard_map/ppermute | solution.py:13
  57.2 21.6 %collective-permute-start.4 = (bf16[2,64,3,2,128]{4,1,3,2,0:T(8,128)(2,1)}, bf16[2,64,3,2,128]{4,1,3,2,0:T(8,128)(2,1)}, u32[]{:S(2)}, u32[]{:S(2)}) collective-permute-start(bf16[2,64,3,2,128]{4,1,3,2,0:T(8,128)(2,1)} %pad_maximum_fusion), channel_id=1, source_target_pairs={{0,4},{4,8},{8,12},{12,16},{16,20},{20,24},{24,28},{28,32},{32,36}... | collective-permute-start | bytes 589832 | tf_op jit(solution)/shard_map/ppermute | solution.py:13
  67.8 0.9 copy-start.8
  67.9 1.0 copy-start.6
  68.0 1.0 copy-start.7
  69.9 18.7 %all-to-all-start = ((bf16[2,64,768]{2,0,1:T(2,128)(2,1)}), bf16[2,64,768]{2,0,1:T(2,128)(2,1)S(1)}, u32[]{:S(2)}, u32[]{:S(2)}) async-start(bf16[2,64,768]{2,0,1:T(2,128)(2,1)} %copy.397), calls=%async_computation | async-start | bytes 393216 | tf_op jit(solution)/shard_map/all_to_all | solution.py:133
  74.2 0.9 copy-start.2
  74.5 4.4 copy-start.5
  76.1 11.4 %copy-start.3 = (f32[1,64,3,256]{3,1,2,0:T(8,128)S(1)}, f32[1,64,3,256]{3,1,2,0:T(8,128)}, u32[]{:S(2)}) copy-start(f32[1,64,3,256]{3,1,2,0:T(8,128)} %fusion.48) | copy-start | bytes 589828
  76.1 11.4 %collective-permute-start.7 = (bf16[2,64,3,256]{3,1,2,0:T(8,128)(2,1)S(1)}, bf16[2,64,3,256]{3,1,2,0:T(8,128)(2,1)S(1)}, u32[]{:S(2)}, u32[]{:S(2)}) collective-permute-start(bf16[2,64,3,256]{3,1,2,0:T(8,128)(2,1)S(1)} %fusion.62), channel_id=1, source_target_pairs={{0,4},{4,8},{8,12},{12,16},{16,20},{20,24},{24,28},{28,32},{32,36}... | collective-permute-start | bytes 589832 | tf_op jit(solution)/shard_map/ppermute | solution.py:13
  79.8 12.3 %collective-permute-start.5 = (bf16[2,64,3,2,128]{4,1,3,2,0:T(8,128)(2,1)S(1)}, bf16[2,64,3,2,128]{4,1,3,2,0:T(8,128)(2,1)S(1)}, u32[]{:S(2)}, u32[]{:S(2)}) collective-permute-start(bf16[2,64,3,2,128]{4,1,3,2,0:T(8,128)(2,1)S(1)} %fusion.60), channel_id=1, source_target_pairs={{0,4},{4,8},{8,12},{12,16},{16,20},{20,24},{24,28},{28,32},{32,36}... | collective-permute-start | bytes 589832 | tf_op jit(solution)/shard_map/ppermute | solution.py:13
  88.6 3.5 copy-start.4
  88.6 7.1 %all-to-all-start.2 = ((bf16[2,64,768]{2,0,1:T(2,128)(2,1)}), bf16[2,64,768]{2,0,1:T(2,128)(2,1)S(1)}, u32[]{:S(2)}, u32[]{:S(2)}) async-start(bf16[2,64,768]{2,0,1:T(2,128)(2,1)} %reshape.427), calls=%async_computation.2 | async-start | bytes 393216 | tf_op jit(solution)/shard_map/all_to_all | solution.py:135
  92.4 8.4 %copy-start.17 = (f32[3]{0:T(128)S(1)}, f32[3]{0:T(128)}, u32[]{:S(2)}) copy-start(f32[3]{0:T(128)} %get-tuple-element.66) | copy-start | bytes 40
  95.7 5.1 %copy-start.18 = (f32[3]{0:T(128)S(1)}, f32[3]{0:T(128)}, u32[]{:S(2)}) copy-start(f32[3]{0:T(128)} %get-tuple-element.52) | copy-start | bytes 40
  95.7 5.1 %copy-start.19 = (f32[3]{0:T(128)S(1)}, f32[3]{0:T(128)}, u32[]{:S(2)}) copy-start(f32[3]{0:T(128)} %get-tuple-element.54) | copy-start | bytes 40
  95.7 5.1 %copy-start.20 = (f32[3]{0:T(128)S(1)}, f32[3]{0:T(128)}, u32[]{:S(2)}) copy-start(f32[3]{0:T(128)} %get-tuple-element.56) | copy-start | bytes 40
  95.7 5.1 %copy-start.21 = (f32[3]{0:T(128)S(1)}, f32[3]{0:T(128)}, u32[]{:S(2)}) copy-start(f32[3]{0:T(128)} %get-tuple-element.58) | copy-start | bytes 40
  95.7 5.1 %copy-start.22 = (f32[3]{0:T(128)S(1)}, f32[3]{0:T(128)}, u32[]{:S(2)}) copy-start(f32[3]{0:T(128)} %get-tuple-element.48) | copy-start | bytes 40
  95.7 5.1 %copy-start.23 = (f32[3]{0:T(128)S(1)}, f32[3]{0:T(128)}, u32[]{:S(2)}) copy-start(f32[3]{0:T(128)} %get-tuple-element.50) | copy-start | bytes 40
  95.7 5.1 %copy-start.24 = (f32[3]{0:T(128)S(1)}, f32[3]{0:T(128)}, u32[]{:S(2)}) copy-start(f32[3]{0:T(128)} %get-tuple-element.46) | copy-start | bytes 40
  95.7 367.2 %all-to-all-start.1 = ((bf16[2,64,768]{2,0,1:T(2,128)(2,1)}), bf16[2,64,768]{2,0,1:T(2,128)(2,1)S(1)}, u32[]{:S(2)}, u32[]{:S(2)}) async-start(bf16[2,64,768]{2,0,1:T(2,128)(2,1)} %reshape.426), calls=%async_computation.1 | async-start | bytes 393216 | tf_op jit(solution)/shard_map/all_to_all | solution.py:134
  100.8 0.7 copy-start.14
  100.8 0.7 copy-start.15
  100.8 0.7 copy-start.16
where the time goes:
time: 464 us
  blocking collectives  360 us (78%)
  starting transfers between devices  50.1 us (11%)
  matrix products  22.1 us (5%)
  local copies, waits for them, and re-layouts  15.6 us (3%)
  waiting for transfers between devices  10 us (2%)
    psum x1, blocking collectives, local(): lambda_grad = lax.psum(lambda_total, 'ctx')  360 us
    ppermute x8, starting transfers between devices, passed_along(): lax.ppermute(shard, axis, [(i, (i + by) % peers) for i in range(peers)])  37.5 us
  transfers between devices with their start and end apart: 11, of which 3 were waited for; matrix products, arithmetic and copies ran while one was open for 6% of the time, Pallas kernels for 0%

commit v1 on v0

v1 whole, which is shorter than its diff:
```python
import functools
import math

import jax
import jax.numpy as jnp
from jax import lax
from jax.experimental import pallas as pl
from jax.experimental.pallas import tpu as pltpu
from jax.sharding import PartitionSpec as P

MESH = pl.DeviceIdType.MESH
F32, BF16 = jnp.float32, jnp.bfloat16
HG = 3
BLK = 64
NH = 4
ROWS = BLK // NH
W = 256
SCALE = 1.0 / math.sqrt(128.0)


def nt(a, b):
    return lax.dot_general(a, b, (((1,), (1,)), ((), ())), preferred_element_type=F32)


def nn(a, b):
    return lax.dot_general(a, b, (((1,), (0,)), ((), ())), preferred_element_type=F32)


def tn(a, b):
    return lax.dot_general(a, b, (((0,), (0,)), ((), ())), preferred_element_type=F32)


def tile_pass(q, do, k, v, rows, lam, mask):
    n0, n1, d0, d1 = rows
    s0 = nt(k[:, :128], q[:, :128])
    s1 = nt(k[:, 128:], q[:, 128:])
    inner = nt(v, do)
    p0 = jnp.where(mask, jnp.exp(s0 * SCALE - n0), 0.0)
    p1 = jnp.where(mask, jnp.exp(s1 * SCALE - n1), 0.0)
    mixed = (p0 - lam * p1).astype(BF16)
    g0 = (SCALE * p0 * (inner - d0)).astype(BF16)
    g1 = ((-lam * SCALE) * p1 * (inner - d1)).astype(BF16)
    dv = nn(mixed, do)
    dk = jnp.concatenate([nn(g0, q[:, :128]), nn(g1, q[:, 128:])], axis=1)
    dq = jnp.concatenate([tn(g0, k[:, :128]), tn(g1, k[:, 128:])], axis=1)
    lam_row = jnp.sum(p1 * inner, axis=0, keepdims=True)
    return dq, dk, dv, lam_row


def kernel(
    n,
    q_hbm, k_hbm, v_hbm, do_hbm, norm_hbm, delta_hbm, lam_ref,
    oq_hbm, ok_hbm, ov_hbm, lam_out,
    q_v, k_v, v_v, do_v, nv, dv_, nd, ndr, rnd, rbuf, wbuf,
    acc_k, acc_v, st_q, st_k, st_v, st_p, st_w, pq, pw, fin_q, lam_tile, lbuf1, lbuf2,
    in_sem, out_sem, qs_send, q_recv, nd_send, nd_recv, ws_send, w_recv,
    r_send, r_recv, p_send, p_recv, pw_send, pw_recv, l_send, l_recv,
):
    me = lax.axis_index("ctx")
    hd = lax.axis_index("head")
    z, r8 = me // 8, me % 8

    def ctx(d):
        return lax.rem(me + (d + n), n)

    def head(d):
        return lax.rem(hd + d, NH)

    loads = [
        pltpu.make_async_copy(a, b, in_sem.at[i])
        for i, (a, b) in enumerate(
            [(q_hbm, q_v), (do_hbm, do_v), (norm_hbm, nv), (delta_hbm, dv_), (k_hbm, k_v), (v_hbm, v_v)]
        )
    ]
    for c in loads:
        c.start()

    barrier = pltpu.get_barrier_semaphore()

    def tell(c, h):
        pl.semaphore_signal(barrier, inc=1, device_id=(c, h), device_id_type=MESH)

    for s in (1, 2):
        tell(ctx(-s), hd)
        for d in range(NH):
            tell(ctx(s), head(d))
    for d in range(1, NH):
        tell(me, head(d))
    for d in range(1, 8):
        tell(z * 8 + lax.rem(r8 + d, 8), hd)
    for d in range(1, 16):
        tell(lax.rem(z + d, 16) * 8 + r8, hd)
    pl.semaphore_wait(barrier, 10 + 3 + 7 + 15)

    loads[0].wait()
    loads[1].wait()
    for g in range(HG):
        cols = pl.ds(g * W, W)
        for s in (1, 2):
            for a, src in enumerate((q_v, do_v)):
                pltpu.make_async_remote_copy(
                    src_ref=src.at[1, :, cols], dst_ref=rbuf.at[g, a, s - 1],
                    send_sem=qs_send.at[s - 1, a], recv_sem=q_recv.at[g],
                    device_id=(ctx(s), hd), device_id_type=MESH,
                ).start()
        if g == 0:
            loads[2].wait()
            loads[3].wait()
            for half in range(2):
                for m in range(2):
                    nd[3 * m : 3 * m + 3, half * 64 : half * 64 + 64] = nv[half, m]
                    nd[8 + 3 * m : 11 + 3 * m, half * 64 : half * 64 + 64] = dv_[half, m]
            for s in (1, 2):
                pltpu.make_async_remote_copy(
                    src_ref=nd, dst_ref=rnd.at[s - 1],
                    send_sem=nd_send.at[s - 1], recv_sem=nd_recv,
                    device_id=(ctx(s), hd), device_id_type=MESH,
                ).start()
    for s in (1, 2):

        @pl.when(me + s >= n)
        def _():
            for g in range(HG):
                for a, src in enumerate((q_v, do_v)):
                    pltpu.make_async_remote_copy(
                        src_ref=src.at[0, :, pl.ds(g * W, W)], dst_ref=wbuf.at[g, a, s - 1],
                        send_sem=ws_send.at[s - 1, a], recv_sem=w_recv.at[s - 1, g],
                        device_id=(ctx(s), hd), device_id_type=MESH,
                    ).start()

    @pl.when(me == 1)
    def _():
        for g in range(HG):
            for a in range(2):
                wbuf[g, a, 0] = jnp.zeros((BLK, W), BF16)

    loads[4].wait()
    loads[5].wait()

    kk = lax.broadcasted_iota(jnp.int32, (128, 128), 0)
    qq = lax.broadcasted_iota(jnp.int32, (128, 128), 1)
    own_mask = ((kk < 64) & (qq >= 64)) | (((kk < 64) == (qq < 64)) & (kk <= qq))
    lim = jnp.where(qq < 64, 1, 2)
    rem_mask = (kk < 64) | (me >= lim)
    wrap_mask = (kk < 64) & (me < lim)

    def rows_of(ref, g):
        return [ref[i : i + 1, :] for i in (g, 3 + g, 8 + g, 11 + g)]

    def kv_of(g):
        cols = pl.ds(g * W, W)
        return k_v[:, :, cols].reshape(128, W), v_v[:, :, cols].reshape(128, W)

    def out_cols(g):
        return pl.ds(pl.multiple_of((hd * HG + g) * W, W), W)

    def rows_at(h):
        return pl.ds(pl.multiple_of(h * ROWS, ROWS), ROWS)

    def spread(stage, dst, g, i):
        for d in range(1, NH):
            pltpu.make_async_remote_copy(
                src_ref=stage.at[g, :, rows_at(head(d)), :], dst_ref=dst.at[:, :, out_cols(g)],
                send_sem=r_send.at[i, g], recv_sem=r_recv.at[i],
                device_id=(me, head(d)), device_id_type=MESH,
            ).start()
        pltpu.make_async_copy(
            stage.at[g, :, rows_at(hd), :], dst.at[:, :, out_cols(g)], out_sem.at[i]
        ).start()

    lam_tile[...] = jnp.zeros((8, 128), F32)
    for g in range(HG):
        cols = pl.ds(g * W, W)
        k, v = kv_of(g)
        q = q_v[:, :, cols].reshape(128, W)
        do = do_v[:, :, cols].reshape(128, W)
        dq, dk, dv, lam_row = tile_pass(q, do, k, v, rows_of(nd, g), lam_ref[g], own_mask)
        st_q[g] = dq.astype(BF16).reshape(2, BLK, W)
        acc_k[g] = dk
        acc_v[g] = dv
        lam_tile[g : g + 1, :] = lam_row
        spread(st_q, pq.at[pl.ds(0, 2)], g, 0)

    def wait_for(ref, sem):
        pltpu.make_async_copy(ref, ref, sem).wait()

    wait_for(rnd, nd_recv)
    left = lax.broadcasted_iota(jnp.int32, (16, 128), 1) < 64
    ndr[0] = jnp.where(left, pltpu.roll(rnd[0], 64, 1), rnd[1])

    @pl.when(me < 2)
    def _():
        ndr[1] = jnp.where(left, rnd[0], pltpu.roll(rnd[1], 64, 1))

    for g in range(HG):
        wait_for(rbuf.at[g], q_recv.at[g])

        for s in (1, 2):

            @pl.when(me < s)
            def _():
                wait_for(wbuf.at[g, :, s - 1], w_recv.at[s - 1, g])

        @pl.when(me < 2)
        def _():
            k, v = kv_of(g)
            dq, dk, dv, lam_row = tile_pass(
                wbuf[g, 0].reshape(128, W), wbuf[g, 1].reshape(128, W), k, v,
                rows_of(ndr.at[1], g), lam_ref[g], wrap_mask,
            )
            st_w[g] = dq.astype(BF16).reshape(2, BLK, W)
            acc_k[g] += dk
            acc_v[g] += dv
            lam_tile[g : g + 1, :] += lam_row

        for s in (1, 2):

            @pl.when(me < s)
            def _():
                for d in range(NH):
                    pltpu.make_async_remote_copy(
                        src_ref=st_w.at[g, s - 1, rows_at(head(d)), :],
                        dst_ref=pw.at[s - 1, :, out_cols(g)],
                        send_sem=pw_send.at[s - 1, g], recv_sem=pw_recv.at[s - 1],
                        device_id=(ctx(-s), head(d)), device_id_type=MESH,
                    ).start()

        k, v = kv_of(g)
        dq, dk, dv, lam_row = tile_pass(
            rbuf[g, 0].reshape(128, W), rbuf[g, 1].reshape(128, W), k, v,
            rows_of(ndr.at[0], g), lam_ref[g], rem_mask,
        )
        st_p[g] = dq.astype(BF16).reshape(2, BLK, W)
        st_k[g] = (acc_k[g] + dk).astype(BF16).reshape(2, BLK, W)
        st_v[g] = (acc_v[g] + dv).astype(BF16).reshape(2, BLK, W)
        lam_tile[g : g + 1, :] += lam_row
        spread(st_k, ok_hbm, g, 1)
        spread(st_v, ov_hbm, g, 2)
        for s in (1, 2):
            for d in range(NH):
                pltpu.make_async_remote_copy(
                    src_ref=st_p.at[g, s - 1, rows_at(head(d)), :],
                    dst_ref=pq.at[s + 1, :, out_cols(g)],
                    send_sem=p_send.at[s - 1, g], recv_sem=p_recv,
                    device_id=(ctx(-s), head(d)), device_id_type=MESH,
                ).start()

    lbuf1[r8] = lam_tile[...]
    for d in range(1, 8):
        pltpu.make_async_remote_copy(
            src_ref=lam_tile, dst_ref=lbuf1.at[r8],
            send_sem=l_send.at[0], recv_sem=l_recv.at[0],
            device_id=(z * 8 + lax.rem(r8 + d, 8), hd), device_id_type=MESH,
        ).start()
    wait_for(lbuf1.at[pl.ds(0, 7)], l_recv.at[0])
    wait_for(lbuf1.at[pl.ds(0, 7)], l_send.at[0])
    total = lbuf1[0]
    for i in range(1, 8):
        total = total + lbuf1[i]
    lam_tile[...] = total
    lbuf2[z] = total
    for d in range(1, 16):
        pltpu.make_async_remote_copy(
            src_ref=lam_tile, dst_ref=lbuf2.at[z],
            send_sem=l_send.at[1], recv_sem=l_recv.at[1],
            device_id=(lax.rem(z + d, 16) * 8 + r8, hd), device_id_type=MESH,
        ).start()
    wait_for(lbuf2.at[pl.ds(0, 15)], l_recv.at[1])
    wait_for(lbuf2.at[pl.ds(0, 15)], l_send.at[1])
    total = lbuf2[0]
    for i in range(1, 16):
        total = total + lbuf2[i]
    lam_out[...] = jnp.broadcast_to(-jnp.sum(total, axis=1, keepdims=True), (8, 128))

    part = pl.ds(0, 3 * HG * W)
    wait_for(pq.at[pl.ds(0, 2), :, part], r_recv.at[0])
    for g in range(HG):
        wait_for(st_q.at[g, :, pl.ds(0, ROWS)], out_sem.at[0])
    wait_for(pq.at[pl.ds(2, 2)], p_recv)
    for s in (1, 2):

        @pl.when(me + s >= n)
        def _():
            wait_for(pw.at[s - 1], pw_recv.at[s - 1])

    fin_q[0] = pq[0]
    fin_q[1] = (pq[1].astype(F32) + pq[2].astype(F32) + pq[3].astype(F32)).astype(BF16)

    @pl.when(me == n - 1)
    def _():
        fin_q[0] = (pq[0].astype(F32) + pw[0].astype(F32) + pw[1].astype(F32)).astype(BF16)

    @pl.when(me == n - 2)
    def _():
        fin_q[0] = (pq[0].astype(F32) + pw[1].astype(F32)).astype(BF16)

    last = pltpu.make_async_copy(fin_q, oq_hbm, out_sem.at[3])
    last.start()

    wait_for(ok_hbm.at[:, :, part], r_recv.at[1])
    wait_for(ov_hbm.at[:, :, part], r_recv.at[2])
    for g in range(HG):
        wait_for(st_k.at[g, :, pl.ds(0, ROWS)], out_sem.at[1])
        wait_for(st_v.at[g, :, pl.ds(0, ROWS)], out_sem.at[2])

    for s in (1, 2):
        for a, src in enumerate((q_v, do_v)):
            wait_for(src.at[1], qs_send.at[s - 1, a])
        wait_for(nd, nd_send.at[s - 1])
        for g in range(HG):
            wait_for(st_p.at[g, s - 1], p_send.at[s - 1, g])

        @pl.when(me + s >= n)
        def _():
            for a, src in enumerate((q_v, do_v)):
                wait_for(src.at[0], ws_send.at[s - 1, a])

        @pl.when(me < s)
        def _():
            for g in range(HG):
                wait_for(st_w.at[g, s - 1], pw_send.at[s - 1, g])

    for i, stage in enumerate((st_q, st_k, st_v)):
        for g in range(HG):
            wait_for(stage.at[g, :, pl.ds(0, 3 * ROWS)], r_send.at[i, g])
    last.wait()


def local(query_rows, key_rows, value_rows, out_grad, log_norms, row_deltas, lambdas):
    n = lax.axis_size("ctx")
    hbm = pl.BlockSpec(memory_space=pl.ANY)
    half = (2, BLK, HG * W)
    out = jax.ShapeDtypeStruct((2, ROWS, NH * HG * W), BF16)
    dma = pltpu.SemaphoreType.DMA
    oq, ok, ov, lam = pl.pallas_call(
        functools.partial(kernel, n),
        out_shape=(out, out, out, jax.ShapeDtypeStruct((8, 128), F32)),
        in_specs=[hbm] * 6 + [pl.BlockSpec(memory_space=pltpu.SMEM)],
        out_specs=(hbm, hbm, hbm, pl.BlockSpec(memory_space=pltpu.VMEM)),
        scratch_shapes=[
            pltpu.VMEM(half, BF16), pltpu.VMEM(half, BF16), pltpu.VMEM(half, BF16), pltpu.VMEM(half, BF16),
            pltpu.VMEM((2, 2, HG, BLK), F32), pltpu.VMEM((2, 2, HG, BLK), F32),
            pltpu.VMEM((16, 128), F32), pltpu.VMEM((2, 16, 128), F32), pltpu.VMEM((2, 16, 128), F32),
            pltpu.VMEM((HG, 2, 2, BLK, W), BF16), pltpu.VMEM((HG, 2, 2, BLK, W), BF16),
            pltpu.VMEM((HG, 2 * BLK, W), F32), pltpu.VMEM((HG, 2 * BLK, W), F32),
            pltpu.VMEM((HG, 2, BLK, W), BF16), pltpu.VMEM((HG, 2, BLK, W), BF16),
            pltpu.VMEM((HG, 2, BLK, W), BF16), pltpu.VMEM((HG, 2, BLK, W), BF16),
            pltpu.VMEM((HG, 2, BLK, W), BF16),
            pltpu.VMEM((4, ROWS, NH * HG * W), BF16), pltpu.VMEM((2, ROWS, NH * HG * W), BF16),
            pltpu.VMEM((2, ROWS, NH * HG * W), BF16),
            pltpu.VMEM((8, 128), F32), pltpu.VMEM((8, 8, 128), F32), pltpu.VMEM((16, 8, 128), F32),
            dma((6,)), dma((4,)), dma((2, 2)), dma((HG,)), dma((2,)), dma, dma((2, 2)), dma((2, HG)),
            dma((3, HG)), dma((3,)), dma((2, HG)), dma, dma((2, HG)), dma((2,)), dma((2,)), dma((2,)),
        ],
        compiler_params=pltpu.CompilerParams(
            collective_id=0, has_side_effects=True, vmem_limit_bytes=32 * 1024 * 1024
        ),
        cost_estimate=pl.CostEstimate(flops=3 * 10**8, bytes_accessed=2 * 10**6, transcendentals=2 * 10**5),
        name="diff_attention_backward",
    )(query_rows, key_rows, value_rows, out_grad, log_norms, row_deltas, lambdas)
    return oq, ok, ov, lam[:HG, 0]


def solution(mesh):
    in_specs = (
        P(None, "ctx", "head"),
        P(None, "ctx", "head"),
        P(None, "ctx", "head"),
        P(None, "ctx", "head"),
        P(None, None, "head", "ctx"),
        P(None, None, "head", "ctx"),
        P("head"),
    )
    out_specs = (
        P(None, ("ctx", "head"), None),
        P(None, ("ctx", "head"), None),
        P(None, ("ctx", "head"), None),
        P("head"),
    )
    return jax.shard_map(local, mesh=mesh, in_specs=in_specs, out_specs=out_specs, check_vma=False)
```

time: 464 us -> 55.8 us (0.12)
  the two profiles are of different devices: /device:TPU:6 before, /device:TPU:32 now
where the time goes in v1:
time: 55.8 us; the launch traced here: 55.5 us
  Pallas kernels  47.2 us (85%)
  local copies, waits for them, and re-layouts  7.72 us (14%)
  between operations  0.66 us (1%)
    pallas_call x1, Pallas kernels, local(): pl.pallas_call(functools.partial(kernel, n), out_shape=(out, out, out, ja...  47.2 us
    unnamed x17, local copies, waits for them, and re-layouts  7.09 us

profile of v1, /device:TPU:32, one launch (start us, length us, event | category | flops | bytes accessed | tf_op | source)
XLA Modules:
  0.0 55.5 jit_solution(14453120614146470395)
XLA Ops:
  0.6 0.0 copy-start.5
  0.6 0.7 %copy.13.norm_hbm = f32[2,2,3,64]{3,2,1,0:T(4,128)S(1)} copy(f32[2,2,3,64]{3,1,2,0:T(2,128)} %param.11) | data formatting | bytes 6144 | tf_op args[4]
  1.3 0.0 copy-done.5
  1.3 0.0 copy-start.4
  1.4 0.6 %copy-done.4 = f32[3]{0:T(128)S(1)} copy-done((f32[3]{0:T(128)S(1)}, f32[3]{0:T(128)}, u32[]{:S(2)}) %copy-start.4) | copy-done | bytes 36
  2.0 0.0 copy-start
  2.0 0.9 %copy-done = bf16[2,64,768]{2,1,0:T(8,128)(2,1)S(1)} copy-done((bf16[2,64,768]{2,1,0:T(8,128)(2,1)S(1)}, bf16[2,64,768]{2,1,0:T(8,128)(2,1)}, u32[]{:S(2)}) %copy-start) | copy-done | bytes 196632
  2.9 0.0 copy-start.1
  2.9 0.9 %copy-done.1 = bf16[2,64,768]{2,1,0:T(8,128)(2,1)S(1)} copy-done((bf16[2,64,768]{2,1,0:T(8,128)(2,1)S(1)}, bf16[2,64,768]{2,1,0:T(8,128)(2,1)}, u32[]{:S(2)}) %copy-start.1) | copy-done | bytes 196632
  3.9 0.0 copy-start.2
  3.9 0.9 %copy-done.2 = bf16[2,64,768]{2,1,0:T(8,128)(2,1)S(1)} copy-done((bf16[2,64,768]{2,1,0:T(8,128)(2,1)S(1)}, bf16[2,64,768]{2,1,0:T(8,128)(2,1)}, u32[]{:S(2)}) %copy-start.2) | copy-done | bytes 196632
  4.8 0.0 copy-start.3
  4.8 0.9 %copy-done.3 = bf16[2,64,768]{2,1,0:T(8,128)(2,1)S(1)} copy-done((bf16[2,64,768]{2,1,0:T(8,128)(2,1)S(1)}, bf16[2,64,768]{2,1,0:T(8,128)(2,1)}, u32[]{:S(2)}) %copy-start.3) | copy-done | bytes 196632
  5.7 47.2 %diff_attention_backward.1 = (bf16[2,16,3072]{2,1,0:T(8,128)(2,1)S(1)}, bf16[2,16,3072]{2,1,0:T(8,128)(2,1)S(1)}, bf16[2,16,3072]{2,1,0:T(8,128)(2,1)S(1)}, f32[8,128]{1,0:T(8,128)S(1)}) custom-call(bf16[2,64,768]{2,1,0:T(8,128)(2,1)S(1)} %copy-done, bf16[2,64,768]{2,1,0:T(8,128)(2,1)S(1)} %copy-done.1, bf16[2,64,768]{2,1,0:T(8,128)(2,1)S(1)} %copy-done.2, ...), custom_call_target="tpu_custom_call" | custom-call | flops 300000000 | bytes 2000000 | tf_op jit(solution)/shard_map/diff_attention_backward/pallas_call | solution.py:335
  52.9 0.6 %slice_reduce_fusion = f32[3]{0:T(128)} fusion(f32[8,128]{1,0:T(8,128)S(1)} %get-tuple-element.11), kind=kLoop, calls=%fused_computation | loop fusion | bytes 24 | tf_op jit(solution)/shard_map/slice | solution.py:361
  53.5 0.7 %copy.18 = bf16[2,16,3072]{2,1,0:T(8,128)(2,1)} copy(bf16[2,16,3072]{2,1,0:T(8,128)(2,1)S(1)} %get-tuple-element.16) | data formatting | bytes 393216
  54.2 0.7 %copy.19 = bf16[2,16,3072]{2,1,0:T(8,128)(2,1)} copy(bf16[2,16,3072]{2,1,0:T(8,128)(2,1)S(1)} %get-tuple-element.17) | data formatting | bytes 393216
  54.9 0.7 %copy.20 = bf16[2,16,3072]{2,1,0:T(8,128)(2,1)} copy(bf16[2,16,3072]{2,1,0:T(8,128)(2,1)S(1)} %get-tuple-element.18) | data formatting | bytes 393216
  (1 shorter events, 0.0 us)
Async XLA Ops:
  0.6 0.7 %copy-start.5 = (f32[2,2,3,64]{3,1,2,0:T(2,128)S(1)}, f32[2,2,3,64]{3,1,2,0:T(2,128)}, u32[]{:S(2)}) copy-start(f32[2,2,3,64]{3,1,2,0:T(2,128)} %param.12) | copy-start | bytes 9220
  1.3 0.7 %copy-start.4 = (f32[3]{0:T(128)S(1)}, f32[3]{0:T(128)}, u32[]{:S(2)}) copy-start(f32[3]{0:T(128)} %lam_ref.1) | copy-start | bytes 40
  2.0 0.9 %copy-start = (bf16[2,64,768]{2,1,0:T(8,128)(2,1)S(1)}, bf16[2,64,768]{2,1,0:T(8,128)(2,1)}, u32[]{:S(2)}) copy-start(bf16[2,64,768]{2,1,0:T(8,128)(2,1)} %q_hbm.1) | copy-start | bytes 589828
  2.9 0.9 %copy-start.1 = (bf16[2,64,768]{2,1,0:T(8,128)(2,1)S(1)}, bf16[2,64,768]{2,1,0:T(8,128)(2,1)}, u32[]{:S(2)}) copy-start(bf16[2,64,768]{2,1,0:T(8,128)(2,1)} %k_hbm.1) | copy-start | bytes 589828
  3.9 0.9 %copy-start.2 = (bf16[2,64,768]{2,1,0:T(8,128)(2,1)S(1)}, bf16[2,64,768]{2,1,0:T(8,128)(2,1)}, u32[]{:S(2)}) copy-start(bf16[2,64,768]{2,1,0:T(8,128)(2,1)} %v_hbm.1) | copy-start | bytes 589828
  4.8 0.9 %copy-start.3 = (bf16[2,64,768]{2,1,0:T(8,128)(2,1)S(1)}, bf16[2,64,768]{2,1,0:T(8,128)(2,1)}, u32[]{:S(2)}) copy-start(bf16[2,64,768]{2,1,0:T(8,128)(2,1)} %do_hbm.1) | copy-start | bytes 589828

commit v2 on v1

v2 whole, which is shorter than its diff:
```python
import functools
import math

import jax
import jax.numpy as jnp
from jax import lax
from jax.experimental import pallas as pl
from jax.experimental.pallas import tpu as pltpu
from jax.sharding import PartitionSpec as P

MESH = pl.DeviceIdType.MESH
F32, BF16 = jnp.float32, jnp.bfloat16
HG = 3
BLK = 64
NH = 4
ROWS = BLK // NH
W = 256
COLS = NH * HG * W
PLANE = 8
DEPTH = 16
SCALE = 1.0 / math.sqrt(128.0)


def nt(a, b):
    return lax.dot_general(a, b, (((1,), (1,)), ((), ())), preferred_element_type=F32)


def nn(a, b):
    return lax.dot_general(a, b, (((1,), (0,)), ((), ())), preferred_element_type=F32)


def tn(a, b):
    return lax.dot_general(a, b, (((0,), (0,)), ((), ())), preferred_element_type=F32)


def tile_pass(q, do, k, v, rows, lam, mask):
    n0, n1, d0, d1 = rows
    s0 = nt(k[:, :128], q[:, :128])
    s1 = nt(k[:, 128:], q[:, 128:])
    inner = nt(v, do)
    p0 = jnp.where(mask, jnp.exp(s0 * SCALE - n0), 0.0)
    p1 = jnp.where(mask, jnp.exp(s1 * SCALE - n1), 0.0)
    mixed = (p0 - lam * p1).astype(BF16)
    g0 = (SCALE * p0 * (inner - d0)).astype(BF16)
    g1 = ((-lam * SCALE) * p1 * (inner - d1)).astype(BF16)
    dv = nn(mixed, do)
    dk = jnp.concatenate([nn(g0, q[:, :128]), nn(g1, q[:, 128:])], axis=1)
    dq = jnp.concatenate([tn(g0, k[:, :128]), tn(g1, k[:, 128:])], axis=1)
    lam_row = jnp.sum(p1 * inner, axis=0, keepdims=True)
    return dq, dk, dv, lam_row


def wait_for(ref, sem):
    pltpu.make_async_copy(ref, ref, sem).wait()


def rounded(x):
    return x.astype(BF16).reshape(2, BLK, W)


def main_kernel(
    n,
    q_hbm, k_hbm, v_hbm, do_hbm, norm_hbm, delta_hbm, lam_hbm,
    pq, lk, lv, lbuf2,
    lam_s, q_v, k_v, v_v, do_v, nv, dv_, nd, ndr, rnd, rbuf, wbuf,
    acc_q, acc_k, acc_v, st_q, st_k, st_v, st_p, st_wk, st_wv, wk, wv, lam_tile, lbuf1,
    in_sem, out_sem, qs_send, q_recv, nd_send, nd_recv, ws_send, w_recv,
    r_send, r_recv, p_send, p_recv, pw_send, pw_recv, l_send, l_recv, line_sem,
):
    me = lax.axis_index("ctx")
    hd = lax.axis_index("head")
    z, r8 = me // PLANE, me % PLANE

    def ctx(d):
        return lax.rem(me + (d + n), n)

    def head(d):
        return lax.rem(hd + d, NH)

    def line(d):
        return lax.rem(z + d, DEPTH) * PLANE + r8

    def ahead(s):
        return me + s < n

    def behind(s):
        return me >= s

    loads = [
        pltpu.make_async_copy(a, b, in_sem.at[i])
        for i, (a, b) in enumerate(
            [(q_hbm, q_v), (do_hbm, do_v), (norm_hbm, nv), (delta_hbm, dv_), (k_hbm, k_v), (v_hbm, v_v), (lam_hbm, lam_s)]
        )
    ]
    for c in loads:
        c.start()

    barrier = pltpu.get_barrier_semaphore()

    def tell(c, h):
        pl.semaphore_signal(barrier, inc=1, device_id=(c, h), device_id_type=MESH)

    for s in (1, 2):
        for d in range(NH):
            tell(ctx(s), head(d))
            tell(ctx(-s), head(d))
    for d in range(1, NH):
        tell(me, head(d))
    for d in range(1, PLANE):
        tell(z * PLANE + lax.rem(r8 + d, PLANE), hd)

    @pl.when(z == 0)
    def _():
        for d in range(1, DEPTH):
            tell(line(d), hd)

    pl.semaphore_wait(barrier, 4 * NH + (NH - 1) + (PLANE - 1) + jnp.where(z > 0, 1, 0))

    @pl.when(z > 0)
    def _():
        pl.semaphore_signal(line_sem.at[0], inc=1, device_id=(r8, hd), device_id_type=MESH)

    loads[0].wait()
    loads[1].wait()
    for g in range(HG):
        cols = pl.ds(g * W, W)
        for s in (1, 2):

            @pl.when(ahead(s))
            def _():
                for a, src in enumerate((q_v, do_v)):
                    pltpu.make_async_remote_copy(
                        src_ref=src.at[1, :, cols], dst_ref=rbuf.at[g, a, s - 1],
                        send_sem=qs_send.at[s - 1, a], recv_sem=q_recv.at[s - 1, g],
                        device_id=(ctx(s), hd), device_id_type=MESH,
                    ).start()
                pass

        if g == 0:
            loads[2].wait()
            loads[3].wait()
            for half in range(2):
                lanes = pl.ds(half * BLK, BLK)
                for i in range(HG):
                    nd[2 * i : 2 * i + 2, lanes] = nv[half, i]
                    nd[8 + 2 * i : 10 + 2 * i, lanes] = dv_[half, i]
            for s in (1, 2):

                @pl.when(ahead(s))
                def _():
                    pltpu.make_async_remote_copy(
                        src_ref=nd, dst_ref=rnd.at[s - 1],
                        send_sem=nd_send.at[s - 1], recv_sem=nd_recv.at[s - 1],
                        device_id=(ctx(s), hd), device_id_type=MESH,
                    ).start()
                    pass

            for c in loads[4:]:
                c.wait()
        for s in (1, 2):

            @pl.when(~behind(s))
            def _():
                for a, src in enumerate((k_v, v_v)):
                    pltpu.make_async_remote_copy(
                        src_ref=src.at[0, :, cols], dst_ref=wbuf.at[g, a, s - 1],
                        send_sem=ws_send.at[s - 1, a], recv_sem=w_recv.at[s - 1, g],
                        device_id=(ctx(-s), hd), device_id_type=MESH,
                    ).start()
                rbuf[g, :, s - 1] = jnp.zeros((2, BLK, W), BF16)
                if g == 0:
                    rnd[s - 1] = jnp.zeros((16, 128), F32)

    @pl.when(me == n - 2)
    def _():
        wbuf[:, :, 0] = jnp.zeros((HG, 2, BLK, W), BF16)

    for s in (1, 2):

        @pl.when(~ahead(s))
        def _():
            pq[s + 1] = jnp.zeros((ROWS, COLS), BF16)

    kk = lax.broadcasted_iota(jnp.int32, (128, 128), 0)
    qq = lax.broadcasted_iota(jnp.int32, (128, 128), 1)
    own_mask = ((kk < 64) & (qq >= 64)) | (((kk < 64) == (qq < 64)) & (kk <= qq))
    rem_mask = (kk < 64) | (qq < 64) | (me >= 2)
    rem_mask = rem_mask & (me >= jnp.where(qq < 64, 1, 2))
    wrap_mask = (kk >= 64) | (me >= n - 1)

    def rows_of(ref, g):
        return [ref[i : i + 1, :] for i in (2 * g, 2 * g + 1, 8 + 2 * g, 9 + 2 * g)]

    def own(ref, g):
        return ref[:, :, pl.ds(g * W, W)].reshape(2 * BLK, W)

    def out_cols(g):
        return pl.ds(pl.multiple_of((hd * HG + g) * W, W), W)

    def rows_at(h):
        return pl.ds(pl.multiple_of(h * ROWS, ROWS), ROWS)

    def spread(stage, dst, g, i):
        for d in range(1, NH):
            pltpu.make_async_remote_copy(
                src_ref=stage.at[g, :, rows_at(head(d)), :], dst_ref=dst.at[:, :, out_cols(g)],
                send_sem=r_send.at[i, g], recv_sem=r_recv.at[i],
                device_id=(me, head(d)), device_id_type=MESH,
            ).start()
        pltpu.make_async_copy(
            stage.at[g, :, rows_at(hd), :], dst.at[:, :, out_cols(g)], out_sem.at[i]
        ).start()

    def give_back(stage, dst, g, c, send, recv):
        for d in range(NH):
            pltpu.make_async_remote_copy(
                src_ref=stage.at[rows_at(head(d)), :], dst_ref=dst.at[:, out_cols(g)],
                send_sem=send, recv_sem=recv,
                device_id=(c, head(d)), device_id_type=MESH,
            ).start()

    own_q = pq.at[pl.ds(0, 2)]
    last_two = me >= n - 2
    lam_tile[...] = jnp.zeros((8, 128), F32)
    for g in range(HG):
        dq, dk, dv, lam_row = tile_pass(
            own(q_v, g), own(do_v, g), own(k_v, g), own(v_v, g), rows_of(nd, g), lam_s[g], own_mask
        )
        st_q[g] = rounded(dq)
        acc_q[g] = dq
        acc_k[g] = dk
        acc_v[g] = dv
        lam_tile[g : g + 1, :] = lam_row

        @pl.when(~last_two)
        def _():
            spread(st_q, own_q, g, 0)

    @pl.when(z == 0)
    def _():
        pl.semaphore_wait(line_sem.at[0], DEPTH - 1)
        for d in range(1, DEPTH):
            pl.semaphore_signal(line_sem.at[1], inc=1, device_id=(line(d), hd), device_id_type=MESH)

    for s in (1, 2):

        @pl.when(behind(s))
        def _():
            wait_for(rnd.at[s - 1], nd_recv.at[s - 1])

    left = lax.broadcasted_iota(jnp.int32, (16, 128), 1) < BLK
    ndr[...] = jnp.where(left, pltpu.roll(rnd[0], BLK, 1), rnd[1])

    for g in range(HG):
        for s in (1, 2):

            @pl.when(behind(s))
            def _():
                wait_for(rbuf.at[g, :, s - 1], q_recv.at[s - 1, g])

        dq, dk, dv, lam_row = tile_pass(
            rbuf[g, 0].reshape(2 * BLK, W), rbuf[g, 1].reshape(2 * BLK, W), own(k_v, g), own(v_v, g),
            rows_of(ndr, g), lam_s[g], rem_mask,
        )
        st_p[g] = rounded(dq)
        st_k[g] = rounded(acc_k[g] + dk)
        st_v[g] = rounded(acc_v[g] + dv)
        lam_tile[g : g + 1, :] += lam_row
        spread(st_k, lk, g, 1)
        spread(st_v, lv, g, 2)
        for s in (1, 2):

            @pl.when(behind(s))
            def _():
                give_back(st_p.at[g, s - 1], pq.at[s + 1], g, ctx(-s), p_send.at[s - 1, g], p_recv.at[s - 1])

        @pl.when(last_two)
        def _():
            for s in (1, 2):

                @pl.when(~ahead(s))
                def _():
                    wait_for(wbuf.at[g, :, s - 1], w_recv.at[s - 1, g])

            dq, dk, dv, lam_row = tile_pass(
                own(q_v, g), own(do_v, g), wbuf[g, 0].reshape(2 * BLK, W), wbuf[g, 1].reshape(2 * BLK, W),
                rows_of(nd, g), lam_s[g], wrap_mask,
            )
            st_q[g] = rounded(acc_q[g] + dq)
            st_wk[g] = rounded(dk)
            st_wv[g] = rounded(dv)
            lam_tile[g : g + 1, :] += lam_row
            for s in (1, 2):

                @pl.when(~ahead(s))
                def _():
                    give_back(st_wk.at[g, s - 1], wk.at[s - 1], g, ctx(s), pw_send.at[s - 1, g, 0], pw_recv.at[s - 1, 0])
                    give_back(st_wv.at[g, s - 1], wv.at[s - 1], g, ctx(s), pw_send.at[s - 1, g, 1], pw_recv.at[s - 1, 1])

            spread(st_q, own_q, g, 0)

    lbuf1[r8] = lam_tile[...]
    for d in range(1, PLANE):
        pltpu.make_async_remote_copy(
            src_ref=lbuf1.at[r8], dst_ref=lbuf1.at[r8],
            send_sem=l_send.at[0], recv_sem=l_recv.at[0],
            device_id=(z * PLANE + lax.rem(r8 + d, PLANE), hd), device_id_type=MESH,
        ).start()

    @pl.when(z > 0)
    def _():
        pl.semaphore_wait(line_sem.at[1], 1)

    wait_for(lbuf1.at[pl.ds(0, PLANE - 1)], l_recv.at[0])
    total = lbuf1[0]
    for i in range(1, PLANE):
        total = total + lbuf1[i]
    lbuf2[z] = total
    for d in range(1, DEPTH):
        pltpu.make_async_remote_copy(
            src_ref=lbuf2.at[z], dst_ref=lbuf2.at[z],
            send_sem=l_send.at[1], recv_sem=l_recv.at[1],
            device_id=(line(d), hd), device_id_type=MESH,
        ).start()

    part = pl.ds(0, (NH - 1) * HG * W)
    for i, (dst, stage) in enumerate(((own_q, st_q), (lk, st_k), (lv, st_v))):
        wait_for(dst.at[:, :, part], r_recv.at[i])
        for g in range(HG):
            wait_for(stage.at[g, :, pl.ds(0, ROWS)], out_sem.at[i])
    for s in (1, 2):

        @pl.when(ahead(s))
        def _():
            wait_for(pq.at[s + 1], p_recv.at[s - 1])

        @pl.when(~behind(s))
        def _():
            for i, (dst, term) in enumerate(((lk, wk), (lv, wv))):
                wait_for(term.at[s - 1], pw_recv.at[s - 1, i])

    @pl.when(me == 0)
    def _():
        for dst, term in ((lk, wk), (lv, wv)):
            dst[0] = (dst[0].astype(F32) + term[0].astype(F32) + term[1].astype(F32)).astype(BF16)

    @pl.when(me == 1)
    def _():
        for dst, term in ((lk, wk), (lv, wv)):
            dst[0] = (dst[0].astype(F32) + term[1].astype(F32)).astype(BF16)


    for s in (1, 2):

        @pl.when(ahead(s))
        def _():
            for a, src in enumerate((q_v, do_v)):
                wait_for(src.at[1], qs_send.at[s - 1, a])
            wait_for(nd, nd_send.at[s - 1])
            pass

        @pl.when(~behind(s))
        def _():
            for a, src in enumerate((k_v, v_v)):
                wait_for(src.at[0], ws_send.at[s - 1, a])
            pass

        for g in range(HG):

            @pl.when(behind(s))
            def _():
                wait_for(st_p.at[g, s - 1], p_send.at[s - 1, g])

            @pl.when(~ahead(s))
            def _():
                wait_for(st_wk.at[g, s - 1], pw_send.at[s - 1, g, 0])
                wait_for(st_wv.at[g, s - 1], pw_send.at[s - 1, g, 1])

    for i, stage in enumerate((st_q, st_k, st_v)):
        for g in range(HG):
            wait_for(stage.at[g, :, pl.ds(0, (NH - 1) * ROWS)], r_send.at[i, g])
    wait_for(lbuf1.at[pl.ds(0, PLANE - 1)], l_send.at[0])
    wait_for(lbuf2.at[pl.ds(0, DEPTH - 1)], l_recv.at[1])
    wait_for(lbuf2.at[pl.ds(0, DEPTH - 1)], l_send.at[1])


def finish_kernel(pq, lk, lv, lbuf2, oq, ok, ov, lam_out, sum_q, sems):
    copies = [
        pltpu.make_async_copy(lk, ok, sems.at[0]),
        pltpu.make_async_copy(lv, ov, sems.at[1]),
        pltpu.make_async_copy(pq.at[0], oq.at[0], sems.at[2]),
        pltpu.make_async_copy(sum_q, oq.at[1], sems.at[3]),
    ]
    for c in copies[:3]:
        c.start()
    sum_q[...] = (pq[1].astype(F32) + pq[2].astype(F32) + pq[3].astype(F32)).astype(BF16)
    copies[3].start()
    total = lbuf2[0]
    for i in range(1, DEPTH):
        total = total + lbuf2[i]
    for g in range(HG):
        lam_out[g] = -jnp.sum(total[g : g + 1, :])
    for c in copies:
        c.wait()


def local(query_rows, key_rows, value_rows, out_grad, log_norms, row_deltas, lambdas):
    n = lax.axis_size("ctx")
    hbm = pl.BlockSpec(memory_space=pl.ANY)
    vmem = pl.BlockSpec(memory_space=pltpu.VMEM)
    smem = pl.BlockSpec(memory_space=pltpu.SMEM)
    half = (2, BLK, HG * W)
    tile = (HG, 2, BLK, W)
    dma, regular = pltpu.SemaphoreType.DMA, pltpu.SemaphoreType.REGULAR
    args = (
        query_rows, key_rows, value_rows, out_grad,
        jnp.swapaxes(log_norms, 1, 2), jnp.swapaxes(row_deltas, 1, 2), lambdas,
    )
    pq, lk, lv, sums = pl.pallas_call(
        functools.partial(main_kernel, n),
        out_shape=(
            pltpu.VMEM((4, ROWS, COLS), BF16),
            pltpu.VMEM((2, ROWS, COLS), BF16), pltpu.VMEM((2, ROWS, COLS), BF16),
            pltpu.VMEM((DEPTH, 8, 128), F32),
        ),
        in_specs=[hbm] * 7,
        out_specs=(vmem,) * 4,
        scratch_shapes=[
            pltpu.SMEM((HG,), F32),
            pltpu.VMEM(half, BF16), pltpu.VMEM(half, BF16), pltpu.VMEM(half, BF16), pltpu.VMEM(half, BF16),
            pltpu.VMEM((2, HG, 2, BLK), F32), pltpu.VMEM((2, HG, 2, BLK), F32),
            pltpu.VMEM((16, 128), F32), pltpu.VMEM((16, 128), F32), pltpu.VMEM((2, 16, 128), F32),
            pltpu.VMEM((HG, 2, 2, BLK, W), BF16), pltpu.VMEM((HG, 2, 2, BLK, W), BF16),
            *[pltpu.VMEM((HG, 2 * BLK, W), F32) for _ in range(3)],
            *[pltpu.VMEM(tile, BF16) for _ in range(6)],
            pltpu.VMEM((2, ROWS, COLS), BF16), pltpu.VMEM((2, ROWS, COLS), BF16),
            pltpu.VMEM((8, 128), F32), pltpu.VMEM((PLANE, 8, 128), F32),
            dma((7,)), dma((3,)), dma((2, 2)), dma((2, HG)), dma((2,)), dma((2,)), dma((2, 2)), dma((2, HG)),
            dma((3, HG)), dma((3,)), dma((2, HG)), dma((2,)), dma((2, HG, 2)), dma((2, 2)), dma((2,)), dma((2,)),
            regular((2,)),
        ],
        compiler_params=pltpu.CompilerParams(
            collective_id=0, has_side_effects=True, vmem_limit_bytes=24 * 1024 * 1024
        ),
        cost_estimate=pl.CostEstimate(flops=3 * 10**8, bytes_accessed=2 * 10**6, transcendentals=2 * 10**5),
        name="attention_backward",
    )(*[pltpu.with_memory_space_constraint(x, pltpu.HBM) for x in args])
    out = jax.ShapeDtypeStruct((2, ROWS, COLS), BF16)
    return pl.pallas_call(
        finish_kernel,
        out_shape=(out, out, out, jax.ShapeDtypeStruct((HG,), F32)),
        in_specs=[vmem] * 4,
        out_specs=(hbm, hbm, hbm, smem),
        scratch_shapes=[pltpu.VMEM((ROWS, COLS), BF16), dma((4,))],
        compiler_params=pltpu.CompilerParams(vmem_limit_bytes=16 * 1024 * 1024),
        name="write_outputs",
    )(*[pltpu.with_memory_space_constraint(x, pltpu.VMEM) for x in (pq, lk, lv, sums)])


def solution(mesh):
    in_specs = (
        P(None, "ctx", "head"),
        P(None, "ctx", "head"),
        P(None, "ctx", "head"),
        P(None, "ctx", "head"),
        P(None, None, "head", "ctx"),
        P(None, None, "head", "ctx"),
        P("head"),
    )
    out_specs = (
        P(None, ("ctx", "head"), None),
        P(None, ("ctx", "head"), None),
        P(None, ("ctx", "head"), None),
        P("head"),
    )
    return jax.shard_map(local, mesh=mesh, in_specs=in_specs, out_specs=out_specs, check_vma=False)
```

time: 55.8 us -> 42 us (0.75)
  the two profiles are of different devices: /device:TPU:32 before, /device:TPU:6 now
where the time goes in v2:
time: 42 us; the launch traced here: 41.8 us
  Pallas kernels  41.1 us (98%)
  between operations  0.64 us (2%)
    pallas_call x1, Pallas kernels, local(): pl.pallas_call(functools.partial(main_kernel, n), out_shape=(pltpu.VMEM((...  39.8 us
    pallas_call x1, Pallas kernels, local(): pl.pallas_call(finish_kernel, out_shape=(out, out, out, jax.ShapeDtypeStr...  1.36 us

profile of v2, /device:TPU:6, one launch (start us, length us, event | category | flops | bytes accessed | tf_op | source)
XLA Modules:
  0.0 41.8 jit_solution(6044098346937520201)
XLA Ops:
  0.6 39.8 %attention_backward.1 = (bf16[4,16,3072]{2,1,0:T(8,128)(2,1)S(1)}, bf16[2,16,3072]{2,1,0:T(8,128)(2,1)S(1)}, bf16[2,16,3072]{2,1,0:T(8,128)(2,1)S(1)}, f32[16,8,128]{2,1,0:T(8,128)S(1)}) custom-call(bf16[2,64,768]{2,1,0:T(8,128)(2,1)} %q_hbm.1, bf16[2,64,768]{2,1,0:T(8,128)(2,1)} %k_hbm.1, bf16[2,64,768]{2,1,0:T(8,128)(2,1)} %v_hbm.1, ...), custom_call_target="tpu_custom_call" | custom-call | flops 300000000 | bytes 2000000 | tf_op jit(solution)/shard_map/attention_backward/pallas_call | solution.py:419
  40.4 1.4 %write_outputs.1 = (bf16[2,16,3072]{2,1,0:T(8,128)(2,1)}, bf16[2,16,3072]{2,1,0:T(8,128)(2,1)}, bf16[2,16,3072]{2,1,0:T(8,128)(2,1)}, f32[3]{0:T(128)}) custom-call(bf16[4,16,3072]{2,1,0:T(8,128)(2,1)S(1)} %get-tuple-element.8.pq, bf16[2,16,3072]{2,1,0:T(8,128)(2,1)S(1)} %get-tuple-element.9.lk, bf16[2,16,3072]{2,1,0:T(8,128)(2,1)S(1)} %get-tuple-element.10.lv, ...), custom_call_target="tpu_custom_call" | custom-call | tf_op jit(solution)/shard_map/write_outputs/pallas_call | solution.py:449

commit v3 on v2

v3 whole, which is shorter than its diff:
```python
import functools
import math

import jax
import jax.numpy as jnp
from jax import lax
from jax.experimental import pallas as pl
from jax.experimental.pallas import tpu as pltpu
from jax.sharding import PartitionSpec as P

MESH = pl.DeviceIdType.MESH
F32, BF16 = jnp.float32, jnp.bfloat16
HG = 3
BLK = 64
NH = 4
ROWS = BLK // NH
W = 256
COLS = NH * HG * W
PLANE = 8
DEPTH = 16
SCALE = 1.0 / math.sqrt(128.0)


def nt(a, b):
    return lax.dot_general(a, b, (((1,), (1,)), ((), ())), preferred_element_type=F32)


def nn(a, b):
    return lax.dot_general(a, b, (((1,), (0,)), ((), ())), preferred_element_type=F32)


def tn(a, b):
    return lax.dot_general(a, b, (((0,), (0,)), ((), ())), preferred_element_type=F32)


def second_map(q1, do, k1, v, rows, mask):
    inner = nt(v, do)
    p1 = jnp.where(mask, jnp.exp(nt(k1, q1) * SCALE - rows[1]), 0.0)
    return p1, inner, jnp.sum(p1 * inner, axis=0, keepdims=True)


def gradients(p1, inner, q0, q1, do, k0, k1, rows, lam, mask):
    n0, _, d0, d1 = rows
    p0 = jnp.where(mask, jnp.exp(nt(k0, q0) * SCALE - n0), 0.0)
    mixed = (p0 - lam * p1).astype(BF16)
    g0 = (SCALE * p0 * (inner - d0)).astype(BF16)
    g1 = ((-lam * SCALE) * p1 * (inner - d1)).astype(BF16)
    dv = nn(mixed, do)
    dk = jnp.concatenate([nn(g0, q0), nn(g1, q1)], axis=1)
    dq = jnp.concatenate([tn(g0, k0), tn(g1, k1)], axis=1)
    return dq, dk, dv


def wait_for(ref, sem):
    pltpu.make_async_copy(ref, ref, sem).wait()


def rounded(x):
    return x.astype(BF16).reshape(2, BLK, W)


def main_kernel(
    n,
    q_hbm, k_hbm, v_hbm, do_hbm, norm_hbm, delta_hbm, lam_hbm,
    pq, lk, lv, lbuf2,
    lam_s, q_v, k_v, v_v, do_v, nv, dv_, nd, ndr, rnd, r_a, r_b, w_a, w_b, h_a, h_b, h_nd,
    r_p1, r_in, w_p1, w_in,
    acc_k, acc_v, st_q, st_k, st_v, st_p, st_wk, st_wv, st_wq, wk, wv, wq, lam_tile, lbuf1,
    in_sem, out_sem, qs_send, a_recv, b_recv, nd_send, nd_recv, ws_send, wa_recv, wb_recv,
    hs_send, ha_recv, hb_recv, hn_recv, wq_send, wq_recv,
    r_send, r_recv, p_send, p_recv, pw_send, pw_recv, l_send, l_recv, line_sem,
):
    me = lax.axis_index("ctx")
    hd = lax.axis_index("head")
    z, r8 = me // PLANE, me % PLANE

    def ctx(d):
        return lax.rem(me + (d + n), n)

    def head(d):
        return lax.rem(hd + d, NH)

    def line(d):
        return lax.rem(z + d, DEPTH) * PLANE + r8

    def ahead(s):
        return me + s < n

    def behind(s):
        return me >= s

    last_two = me >= n - 2
    host = (me >= PLANE - 2) & (me < PLANE)
    guest = me + (n - PLANE)

    def hosts(s):
        return host & (me + s >= PLANE)

    loads = [
        pltpu.make_async_copy(a, b, in_sem.at[i])
        for i, (a, b) in enumerate(
            [(q_hbm, q_v), (do_hbm, do_v), (norm_hbm, nv), (delta_hbm, dv_), (k_hbm, k_v), (v_hbm, v_v), (lam_hbm, lam_s)]
        )
    ]
    for c in loads:
        c.start()

    barrier = pltpu.get_barrier_semaphore()

    def tell(c, h):
        pl.semaphore_signal(barrier, inc=1, device_id=(c, h), device_id_type=MESH)

    heads = range(NH)
    for s in (1, 2):

        @pl.when(ahead(s))
        def _():
            for d in heads:
                tell(ctx(s), head(d))

        @pl.when(behind(s))
        def _():
            for d in heads:
                tell(ctx(-s), head(d))

        @pl.when(~behind(s))
        def _():
            for d in heads:
                tell(me - s + PLANE, head(d))

    for d in range(1, NH):
        tell(me, head(d))
    for d in range(1, PLANE):
        tell(z * PLANE + lax.rem(r8 + d, PLANE), hd)

    @pl.when(z == 0)
    def _():
        for d in range(1, DEPTH):
            tell(line(d), hd)

    @pl.when(host)
    def _():
        for d in range(1, NH):
            tell(guest, head(d))

    def when(condition, count):
        return jnp.where(condition, count, 0)

    pl.semaphore_wait(
        barrier,
        sum(when(ahead(s), NH) + when(behind(s), NH) + when(hosts(s), NH) for s in (1, 2))
        + when(z > 0, 1) + when(last_two, NH - 1) + (NH - 1) + (PLANE - 1),
    )

    @pl.when(z > 0)
    def _():
        pl.semaphore_signal(line_sem.at[0], inc=1, device_id=(r8, hd), device_id_type=MESH)

    @pl.when(last_two)
    def _():
        for d in heads:
            pl.semaphore_signal(line_sem.at[2], inc=1, device_id=(r8, head(d)), device_id_type=MESH)

    def map_cols(g, m):
        return pl.ds(g * W + m * 128, 128)

    def send_first(src, wide, half, dst, g, s, c, send, recv):
        for i, (ref, cols, lanes) in enumerate(
            ((src, map_cols(g, 1), pl.ds(0, 128)), (wide, pl.ds(g * W, W), pl.ds(128, W)))
        ):
            pltpu.make_async_remote_copy(
                src_ref=ref.at[half, :, cols], dst_ref=dst.at[g, s - 1, :, lanes],
                send_sem=send.at[s - 1, i], recv_sem=recv.at[s - 1, g],
                device_id=(c, hd), device_id_type=MESH,
            ).start()

    def send_second(src, half, dst, g, s, c, send, recv):
        pltpu.make_async_remote_copy(
            src_ref=src.at[half, :, map_cols(g, 0)], dst_ref=dst.at[g, s - 1],
            send_sem=send.at[s - 1, 2], recv_sem=recv.at[s - 1, g],
            device_id=(c, hd), device_id_type=MESH,
        ).start()

    loads[0].wait()
    loads[1].wait()

    @pl.when(last_two)
    def _():
        for g in range(HG):
            for i, (ref, cols, lanes) in enumerate(
                ((q_v, map_cols(g, 1), pl.ds(0, 128)), (do_v, pl.ds(g * W, W), pl.ds(128, W)))
            ):
                pltpu.make_async_remote_copy(
                    src_ref=ref.at[:, :, cols], dst_ref=h_a.at[g, :, :, lanes],
                    send_sem=hs_send.at[i], recv_sem=ha_recv.at[g],
                    device_id=(r8, hd), device_id_type=MESH,
                ).start()

    for g in range(HG):
        for s in (1, 2):

            @pl.when(ahead(s))
            def _():
                send_first(q_v, do_v, 1, r_a, g, s, ctx(s), qs_send, a_recv)

    for c in loads[2:]:
        c.wait()
    for half in range(2):
        lanes = pl.ds(half * BLK, BLK)
        for i in range(HG):
            nd[2 * i : 2 * i + 2, lanes] = nv[half, i]
            nd[8 + 2 * i : 10 + 2 * i, lanes] = dv_[half, i]
    for s in (1, 2):

        @pl.when(ahead(s))
        def _():
            pltpu.make_async_remote_copy(
                src_ref=nd, dst_ref=rnd.at[s - 1],
                send_sem=nd_send.at[s - 1], recv_sem=nd_recv.at[s - 1],
                device_id=(ctx(s), hd), device_id_type=MESH,
            ).start()

        @pl.when(~behind(s))
        def _():
            for g in range(HG):
                send_first(k_v, v_v, 0, w_a, g, s, me - s + PLANE, ws_send, wa_recv)

    @pl.when(last_two)
    def _():
        pltpu.make_async_remote_copy(
            src_ref=nd, dst_ref=h_nd, send_sem=hs_send.at[2], recv_sem=hn_recv,
            device_id=(r8, hd), device_id_type=MESH,
        ).start()
        for g in range(HG):
            pltpu.make_async_remote_copy(
                src_ref=q_v.at[:, :, map_cols(g, 0)], dst_ref=h_b.at[g],
                send_sem=hs_send.at[3], recv_sem=hb_recv.at[g],
                device_id=(r8, hd), device_id_type=MESH,
            ).start()

    for s in (1, 2):

        @pl.when(ahead(s))
        def _():
            for g in range(HG):
                send_second(q_v, 1, r_b, g, s, ctx(s), qs_send, b_recv)

        @pl.when(~behind(s))
        def _():
            for g in range(HG):
                send_second(k_v, 0, w_b, g, s, me - s + PLANE, ws_send, wb_recv)


    for s in (1, 2):

        @pl.when(~behind(s))
        def _():
            r_a[:, s - 1] = jnp.zeros((HG, BLK, 128 + W), BF16)
            r_b[:, s - 1] = jnp.zeros((HG, BLK, 128), BF16)
            rnd[s - 1] = jnp.zeros((16, 128), F32)

    @pl.when(me == PLANE - 2)
    def _():
        w_a[:, 0] = jnp.zeros((HG, BLK, 128 + W), BF16)
        w_b[:, 0] = jnp.zeros((HG, BLK, 128), BF16)

    @pl.when(me == n - 1)
    def _():
        pq[2] = jnp.zeros((ROWS, COLS), BF16)

    kk = lax.broadcasted_iota(jnp.int32, (128, 128), 0)
    qq = lax.broadcasted_iota(jnp.int32, (128, 128), 1)
    own_mask = ((kk < 64) & (qq >= 64)) | (((kk < 64) == (qq < 64)) & (kk <= qq))
    rem_mask = (kk < 64) | (qq < 64) | (me >= 2)
    rem_mask = rem_mask & (me >= jnp.where(qq < 64, 1, 2))
    wrap_mask = (kk >= 64) | (me == PLANE - 1)

    def rows_of(ref, g):
        return [ref[i : i + 1, :] for i in (2 * g, 2 * g + 1, 8 + 2 * g, 9 + 2 * g)]

    def own(ref, g):
        return ref[:, :, pl.ds(g * W, W)].reshape(2 * BLK, W)

    def own_map(ref, g, m):
        return ref[:, :, map_cols(g, m)].reshape(2 * BLK, 128)

    def first(ref, g):
        both = ref[g].reshape(2 * BLK, 128 + W)
        return both[:, :128], both[:, 128:]

    def second(ref, g):
        return ref[g].reshape(2 * BLK, 128)

    def out_cols(g):
        return pl.ds(pl.multiple_of((hd * HG + g) * W, W), W)

    def rows_at(h):
        return pl.ds(pl.multiple_of(h * ROWS, ROWS), ROWS)

    def spread(stage, dst, g, i):
        for d in range(1, NH):
            pltpu.make_async_remote_copy(
                src_ref=stage.at[g, :, rows_at(head(d)), :], dst_ref=dst.at[:, :, out_cols(g)],
                send_sem=r_send.at[i, g], recv_sem=r_recv.at[i],
                device_id=(me, head(d)), device_id_type=MESH,
            ).start()
        pltpu.make_async_copy(
            stage.at[g, :, rows_at(hd), :], dst.at[:, :, out_cols(g)], out_sem.at[i]
        ).start()

    def give_back(stage, dst, g, c, send, recv):
        for d in range(NH):
            pltpu.make_async_remote_copy(
                src_ref=stage.at[rows_at(head(d)), :], dst_ref=dst.at[:, out_cols(g)],
                send_sem=send, recv_sem=recv,
                device_id=(c, head(d)), device_id_type=MESH,
            ).start()

    own_q = pq.at[pl.ds(0, 2)]
    lam_tile[...] = jnp.zeros((8, 128), F32)
    for g in range(HG):
        q0, q1, do = own_map(q_v, g, 0), own_map(q_v, g, 1), own(do_v, g)
        k0, k1, v = own_map(k_v, g, 0), own_map(k_v, g, 1), own(v_v, g)
        p1, inner, lam_row = second_map(q1, do, k1, v, rows_of(nd, g), own_mask)
        dq, dk, dv = gradients(p1, inner, q0, q1, do, k0, k1, rows_of(nd, g), lam_s[g], own_mask)
        st_q[g] = rounded(dq)
        acc_k[g] = dk
        acc_v[g] = dv
        lam_tile[g : g + 1, :] = lam_row
        spread(st_q, own_q, g, 0)

    for s in (1, 2):

        @pl.when(behind(s))
        def _():
            wait_for(rnd.at[s - 1], nd_recv.at[s - 1])

    left = lax.broadcasted_iota(jnp.int32, (16, 128), 1) < BLK
    ndr[...] = jnp.where(left, pltpu.roll(rnd[0], BLK, 1), rnd[1])

    for g in range(HG):
        for s in (1, 2):

            @pl.when(behind(s))
            def _():
                wait_for(r_a.at[g, s - 1], a_recv.at[s - 1, g])

        q1, do = first(r_a, g)
        r_p1[g], r_in[g], lam_row = second_map(q1, do, own_map(k_v, g, 1), own(v_v, g), rows_of(ndr, g), rem_mask)
        lam_tile[g : g + 1, :] += lam_row

    @pl.when(z == 0)
    def _():
        pl.semaphore_wait(line_sem.at[0], DEPTH - 1)
        for d in range(1, DEPTH):
            pl.semaphore_signal(line_sem.at[1], inc=1, device_id=(line(d), hd), device_id_type=MESH)

    def sum_over_plane():
        lbuf1[r8] = lam_tile[...]
        for d in range(1, PLANE):
            pltpu.make_async_remote_copy(
                src_ref=lbuf1.at[r8], dst_ref=lbuf1.at[r8],
                send_sem=l_send.at[0], recv_sem=l_recv.at[0],
                device_id=(z * PLANE + lax.rem(r8 + d, PLANE), hd), device_id_type=MESH,
            ).start()
        pass

    def sum_over_line():
        @pl.when(z > 0)
        def _():
            pl.semaphore_wait(line_sem.at[1], 1)

        wait_for(lbuf1.at[pl.ds(0, PLANE - 1)], l_recv.at[0])
        total = lbuf1[0]
        for i in range(1, PLANE):
            total = total + lbuf1[i]
        lbuf2[z] = total
        for d in range(1, DEPTH):
            pltpu.make_async_remote_copy(
                src_ref=lbuf2.at[z], dst_ref=lbuf2.at[z],
                send_sem=l_send.at[1], recv_sem=l_recv.at[1],
                device_id=(line(d), hd), device_id_type=MESH,
            ).start()

    @pl.when(z > 0)
    def _():
        sum_over_plane()

    for g in range(HG):
        for s in (1, 2):

            @pl.when(behind(s))
            def _():
                wait_for(r_b.at[g, s - 1], b_recv.at[s - 1, g])

        q1, do = first(r_a, g)
        dq, dk, dv = gradients(
            r_p1[g], r_in[g], second(r_b, g), q1, do, own_map(k_v, g, 0), own_map(k_v, g, 1),
            rows_of(ndr, g), lam_s[g], rem_mask,
        )
        st_p[g] = rounded(dq)
        st_k[g] = rounded(acc_k[g] + dk)
        st_v[g] = rounded(acc_v[g] + dv)
        for s in (1, 2):

            @pl.when(behind(s))
            def _():
                give_back(st_p.at[g, s - 1], pq.at[s + 1], g, ctx(-s), p_send.at[s - 1, g], p_recv.at[s - 1])

        spread(st_k, lk, g, 1)
        spread(st_v, lv, g, 2)
        if g == 1:

            @pl.when(z > 0)
            def _():
                sum_over_line()

    @pl.when(host)
    def _():
        wait_for(h_nd, hn_recv)
        for g in range(HG):
            wait_for(h_a.at[g], ha_recv.at[g])
            for s in (1, 2):

                @pl.when(hosts(s))
                def _():
                    wait_for(w_a.at[g, s - 1], wa_recv.at[s - 1, g])

            q1, do = first(h_a, g)
            k1, v = first(w_a, g)
            w_p1[g], w_in[g], lam_row = second_map(q1, do, k1, v, rows_of(h_nd, g), wrap_mask)
            lam_tile[g : g + 1, :] += lam_row

    @pl.when(z == 0)
    def _():
        sum_over_plane()

    @pl.when(host)
    def _():
        pl.semaphore_wait(line_sem.at[2], NH)
        for g in range(HG):
            wait_for(h_b.at[g], hb_recv.at[g])
            for s in (1, 2):

                @pl.when(hosts(s))
                def _():
                    wait_for(w_b.at[g, s - 1], wb_recv.at[s - 1, g])

            q1, do = first(h_a, g)
            k1, v = first(w_a, g)
            dq, dk, dv = gradients(
                w_p1[g], w_in[g], second(h_b, g), q1, do, second(w_b, g), k1, rows_of(h_nd, g), lam_s[g], wrap_mask
            )
            st_wq[g] = rounded(dq)
            st_wk[g] = rounded(dk)
            st_wv[g] = rounded(dv)
            for d in heads:
                pltpu.make_async_remote_copy(
                    src_ref=st_wq.at[g, :, rows_at(head(d)), :], dst_ref=wq.at[:, :, out_cols(g)],
                    send_sem=wq_send.at[g], recv_sem=wq_recv,
                    device_id=(guest, head(d)), device_id_type=MESH,
                ).start()
            for s in (1, 2):

                @pl.when(hosts(s))
                def _():
                    to = me + s - PLANE
                    give_back(st_wk.at[g, s - 1], wk.at[s - 1], g, to, pw_send.at[s - 1, g, 0], pw_recv.at[s - 1, 0])
                    give_back(st_wv.at[g, s - 1], wv.at[s - 1], g, to, pw_send.at[s - 1, g, 1], pw_recv.at[s - 1, 1])

    @pl.when(z == 0)
    def _():
        sum_over_line()

    part = pl.ds(0, (NH - 1) * HG * W)
    for i, (dst, stage) in enumerate(((own_q, st_q), (lk, st_k), (lv, st_v))):
        wait_for(dst.at[:, :, part], r_recv.at[i])
        for g in range(HG):
            wait_for(stage.at[g, :, pl.ds(0, ROWS)], out_sem.at[i])
    for s in (1, 2):

        @pl.when(ahead(s))
        def _():
            wait_for(pq.at[s + 1], p_recv.at[s - 1])

        @pl.when(~behind(s))
        def _():
            for i, (dst, term) in enumerate(((lk, wk), (lv, wv))):
                wait_for(term.at[s - 1], pw_recv.at[s - 1, i])

    @pl.when(me == 0)
    def _():
        for dst, term in ((lk, wk), (lv, wv)):
            dst[0] = (dst[0].astype(F32) + term[0].astype(F32) + term[1].astype(F32)).astype(BF16)

    @pl.when(me == 1)
    def _():
        for dst, term in ((lk, wk), (lv, wv)):
            dst[0] = (dst[0].astype(F32) + term[1].astype(F32)).astype(BF16)

    @pl.when(last_two)
    def _():
        wait_for(wq, wq_recv)
        pq[0] = (pq[0].astype(F32) + wq[0].astype(F32)).astype(BF16)
        pq[3] = wq[1]


    sent = (q_v.at[0, :, pl.ds(0, HG * 128)], q_v.at[0])
    for s in (1, 2):

        @pl.when(ahead(s))
        def _():
            wait_for(sent[0], qs_send.at[s - 1, 0])
            wait_for(sent[1], qs_send.at[s - 1, 1])
            wait_for(sent[0], qs_send.at[s - 1, 2])
            wait_for(nd, nd_send.at[s - 1])
            pass

        @pl.when(~behind(s))
        def _():
            wait_for(sent[0], ws_send.at[s - 1, 0])
            wait_for(sent[1], ws_send.at[s - 1, 1])
            wait_for(sent[0], ws_send.at[s - 1, 2])
            pass

        for g in range(HG):

            @pl.when(behind(s))
            def _():
                wait_for(st_p.at[g, s - 1], p_send.at[s - 1, g])

            @pl.when(hosts(s))
            def _():
                wait_for(st_wk.at[g, s - 1], pw_send.at[s - 1, g, 0])
                wait_for(st_wv.at[g, s - 1], pw_send.at[s - 1, g, 1])

    @pl.when(host)
    def _():
        for g in range(HG):
            wait_for(st_wq.at[g], wq_send.at[g])
        pass

    @pl.when(last_two)
    def _():
        both = q_v.at[:, :, pl.ds(0, HG * 128)]
        wait_for(both, hs_send.at[0])
        wait_for(q_v, hs_send.at[1])
        wait_for(nd, hs_send.at[2])
        wait_for(both, hs_send.at[3])
        pass

    for i, stage in enumerate((st_q, st_k, st_v)):
        for g in range(HG):
            wait_for(stage.at[g, :, pl.ds(0, (NH - 1) * ROWS)], r_send.at[i, g])
    wait_for(lbuf1.at[pl.ds(0, PLANE - 1)], l_send.at[0])
    wait_for(lbuf2.at[pl.ds(0, DEPTH - 1)], l_recv.at[1])
    wait_for(lbuf2.at[pl.ds(0, DEPTH - 1)], l_send.at[1])


def finish_kernel(pq, lk, lv, lbuf2, oq, ok, ov, lam_out, sum_q, sems):
    copies = [
        pltpu.make_async_copy(lk, ok, sems.at[0]),
        pltpu.make_async_copy(lv, ov, sems.at[1]),
        pltpu.make_async_copy(pq.at[0], oq.at[0], sems.at[2]),
        pltpu.make_async_copy(sum_q, oq.at[1], sems.at[3]),
    ]
    for c in copies[:3]:
        c.start()
    sum_q[...] = (pq[1].astype(F32) + pq[2].astype(F32) + pq[3].astype(F32)).astype(BF16)
    copies[3].start()
    total = lbuf2[0]
    for i in range(1, DEPTH):
        total = total + lbuf2[i]
    for g in range(HG):
        lam_out[g] = -jnp.sum(total[g : g + 1, :])
    for c in copies:
        c.wait()


def local(query_rows, key_rows, value_rows, out_grad, log_norms, row_deltas, lambdas):
    n = lax.axis_size("ctx")
    hbm = pl.BlockSpec(memory_space=pl.ANY)
    vmem = pl.BlockSpec(memory_space=pltpu.VMEM)
    smem = pl.BlockSpec(memory_space=pltpu.SMEM)
    half = (2, BLK, HG * W)
    tile = (HG, 2, BLK, W)
    dma, regular = pltpu.SemaphoreType.DMA, pltpu.SemaphoreType.REGULAR
    args = (
        query_rows, key_rows, value_rows, out_grad,
        jnp.swapaxes(log_norms, 1, 2), jnp.swapaxes(row_deltas, 1, 2), lambdas,
    )
    pq, lk, lv, sums = pl.pallas_call(
        functools.partial(main_kernel, n),
        out_shape=(
            pltpu.VMEM((4, ROWS, COLS), BF16),
            pltpu.VMEM((2, ROWS, COLS), BF16), pltpu.VMEM((2, ROWS, COLS), BF16),
            pltpu.VMEM((DEPTH, 8, 128), F32),
        ),
        in_specs=[hbm] * 7,
        out_specs=(vmem,) * 4,
        scratch_shapes=[
            pltpu.SMEM((HG,), F32),
            pltpu.VMEM(half, BF16), pltpu.VMEM(half, BF16), pltpu.VMEM(half, BF16), pltpu.VMEM(half, BF16),
            pltpu.VMEM((2, HG, 2, BLK), F32), pltpu.VMEM((2, HG, 2, BLK), F32),
            pltpu.VMEM((16, 128), F32), pltpu.VMEM((16, 128), F32), pltpu.VMEM((2, 16, 128), F32),
            *[pltpu.VMEM((HG, 2, BLK, c), BF16) for c in (128 + W, 128) * 3],
            pltpu.VMEM((16, 128), F32),
            *[pltpu.VMEM((HG, 2 * BLK, 2 * BLK), F32) for _ in range(4)],
            *[pltpu.VMEM((HG, 2 * BLK, W), F32) for _ in range(2)],
            *[pltpu.VMEM(tile, BF16) for _ in range(7)],
            *[pltpu.VMEM((2, ROWS, COLS), BF16) for _ in range(3)],
            pltpu.VMEM((8, 128), F32), pltpu.VMEM((PLANE, 8, 128), F32),
            dma((7,)), dma((3,)), dma((2, 3)), dma((2, HG)), dma((2, HG)), dma((2,)), dma((2,)),
            dma((2, 3)), dma((2, HG)), dma((2, HG)),
            dma((4,)), dma((HG,)), dma((HG,)), dma, dma((HG,)), dma,
            dma((3, HG)), dma((3,)), dma((2, HG)), dma((2,)), dma((2, HG, 2)), dma((2, 2)), dma((2,)), dma((2,)),
            regular((3,)),
        ],
        compiler_params=pltpu.CompilerParams(
            collective_id=0, has_side_effects=True, vmem_limit_bytes=24 * 1024 * 1024
        ),
        cost_estimate=pl.CostEstimate(flops=3 * 10**8, bytes_accessed=2 * 10**6, transcendentals=2 * 10**5),
        name="attention_backward",
    )(*[pltpu.with_memory_space_constraint(x, pltpu.HBM) for x in args])
    out = jax.ShapeDtypeStruct((2, ROWS, COLS), BF16)
    return pl.pallas_call(
        finish_kernel,
        out_shape=(out, out, out, jax.ShapeDtypeStruct((HG,), F32)),
        in_specs=[vmem] * 4,
        out_specs=(hbm, hbm, hbm, smem),
        scratch_shapes=[pltpu.VMEM((ROWS, COLS), BF16), dma((4,))],
        compiler_params=pltpu.CompilerParams(vmem_limit_bytes=16 * 1024 * 1024),
        name="write_outputs",
    )(*[pltpu.with_memory_space_constraint(x, pltpu.VMEM) for x in (pq, lk, lv, sums)])


def solution(mesh):
    in_specs = (
        P(None, "ctx", "head"),
        P(None, "ctx", "head"),
        P(None, "ctx", "head"),
        P(None, "ctx", "head"),
        P(None, None, "head", "ctx"),
        P(None, None, "head", "ctx"),
        P("head"),
    )
    out_specs = (
        P(None, ("ctx", "head"), None),
        P(None, ("ctx", "head"), None),
        P(None, ("ctx", "head"), None),
        P("head"),
    )
    return jax.shard_map(local, mesh=mesh, in_specs=in_specs, out_specs=out_specs, check_vma=False)
```

time: 42 us -> 39.5 us (0.940)
  Pallas kernels: 41.1 us -> 38.5 us
    pallas_call x1, Pallas kernels: 39.8 us -> 37.2 us  [local(): pl.pallas_call(functools.partial(main_kernel, n), out_shape=(pltpu.VMEM((...]
where the time goes in v3:
time: 39.5 us; the launch traced here: 39.2 us
  Pallas kernels  38.5 us (97%)
  between operations  0.64 us (2%)
    pallas_call x1, Pallas kernels, local(): pl.pallas_call(functools.partial(main_kernel, n), out_shape=(pltpu.VMEM((...  37.2 us
    pallas_call x1, Pallas kernels, local(): pl.pallas_call(finish_kernel, out_shape=(out, out, out, jax.ShapeDtypeStr...  1.36 us

profile of v3, /device:TPU:6, one launch (start us, length us, event | category | flops | bytes accessed | tf_op | source)
XLA Modules:
  0.0 39.2 jit_solution(173989801826605006)
XLA Ops:
  0.6 37.2 %attention_backward.1 = (bf16[4,16,3072]{2,1,0:T(8,128)(2,1)S(1)}, bf16[2,16,3072]{2,1,0:T(8,128)(2,1)S(1)}, bf16[2,16,3072]{2,1,0:T(8,128)(2,1)S(1)}, f32[16,8,128]{2,1,0:T(8,128)S(1)}) custom-call(bf16[2,64,768]{2,1,0:T(8,128)(2,1)} %q_hbm.1, bf16[2,64,768]{2,1,0:T(8,128)(2,1)} %k_hbm.1, bf16[2,64,768]{2,1,0:T(8,128)(2,1)} %v_hbm.1, ...), custom_call_target="tpu_custom_call" | custom-call | flops 300000000 | bytes 2000000 | tf_op jit(solution)/shard_map/attention_backward/pallas_call | solution.py:592
  37.8 1.4 %write_outputs.1 = (bf16[2,16,3072]{2,1,0:T(8,128)(2,1)}, bf16[2,16,3072]{2,1,0:T(8,128)(2,1)}, bf16[2,16,3072]{2,1,0:T(8,128)(2,1)}, f32[3]{0:T(128)}) custom-call(bf16[4,16,3072]{2,1,0:T(8,128)(2,1)S(1)} %get-tuple-element.8.pq, bf16[2,16,3072]{2,1,0:T(8,128)(2,1)S(1)} %get-tuple-element.9.lk, bf16[2,16,3072]{2,1,0:T(8,128)(2,1)S(1)} %get-tuple-element.10.lv, ...), custom_call_target="tpu_custom_call" | custom-call | tf_op jit(solution)/shard_map/write_outputs/pallas_call | solution.py:626

commit v4 on v3

v4 whole, which is shorter than its diff:
```python
import functools
import math

import jax
import jax.numpy as jnp
from jax import lax
from jax.experimental import pallas as pl
from jax.experimental.pallas import tpu as pltpu
from jax.sharding import PartitionSpec as P

MESH = pl.DeviceIdType.MESH
F32, BF16 = jnp.float32, jnp.bfloat16
HG = 3
BLK = 64
NH = 4
ROWS = BLK // NH
W = 256
COLS = NH * HG * W
PLANE = 8
DEPTH = 16
EARLY = 4
SCALE = 1.0 / math.sqrt(128.0)


def nt(a, b):
    return lax.dot_general(a, b, (((1,), (1,)), ((), ())), preferred_element_type=F32)


def nn(a, b):
    return lax.dot_general(a, b, (((1,), (0,)), ((), ())), preferred_element_type=F32)


def tn(a, b):
    return lax.dot_general(a, b, (((0,), (0,)), ((), ())), preferred_element_type=F32)


def second_map(q1, do, k1, v, rows, mask):
    inner = nt(v, do)
    p1 = jnp.where(mask, jnp.exp(nt(k1, q1) * SCALE - rows[1]), 0.0)
    return p1, inner, jnp.sum(p1 * inner, axis=0, keepdims=True)


def gradients(p1, inner, q0, q1, do, k0, k1, rows, lam, mask):
    n0, _, d0, d1 = rows
    p0 = jnp.where(mask, jnp.exp(nt(k0, q0) * SCALE - n0), 0.0)
    mixed = (p0 - lam * p1).astype(BF16)
    g0 = (SCALE * p0 * (inner - d0)).astype(BF16)
    g1 = ((-lam * SCALE) * p1 * (inner - d1)).astype(BF16)
    dv = nn(mixed, do)
    dk = jnp.concatenate([nn(g0, q0), nn(g1, q1)], axis=1)
    dq = jnp.concatenate([tn(g0, k0), tn(g1, k1)], axis=1)
    return dq, dk, dv


def wait_for(ref, sem):
    pltpu.make_async_copy(ref, ref, sem).wait()


def rounded(x):
    return x.astype(BF16).reshape(2, BLK, W)


def main_kernel(
    n,
    q_hbm, k_hbm, v_hbm, do_hbm, norm_hbm, delta_hbm, lam_hbm,
    landed, back, lbuf2,
    lam_s, q_v, k_v, v_v, do_v, nv, dv_, nd, ndr, rnd, r_a, r_b, w_kv, h_qd, h_nd, r_p1, r_in,
    acc, stage, st_p, st_wkv, st_wq, wkv, wq, lam_tile, lbuf1,
    in_sem, own_sem, qs_send, a_recv, b_recv, f_send, nd_send, nd_recv, ws_send, w_recv,
    hs_send, h_recv, hn_recv, wq_send, wq_recv,
    r_send, r_recv, p_send, p_recv, pw_send, pw_recv, l_send, l_recv, line_sem,
):
    me = lax.axis_index("ctx")
    hd = lax.axis_index("head")
    z, r8 = me // PLANE, me % PLANE

    def ctx(d):
        return lax.rem(me + (d + n), n)

    def head(d):
        return lax.rem(hd + d, NH)

    def line(d):
        return lax.rem(z + d, DEPTH) * PLANE + r8

    def ahead(s):
        return me + s < n

    def behind(s):
        return me >= s

    last_two = me >= n - 2
    host = (me >= PLANE - 2) & (me < PLANE)
    guest = me + (n - PLANE)

    def hosts(s):
        return host & (me + s >= PLANE)

    loads = [
        pltpu.make_async_copy(a, b, in_sem.at[i])
        for i, (a, b) in enumerate(
            [(q_hbm, q_v), (do_hbm, do_v), (norm_hbm, nv), (delta_hbm, dv_), (k_hbm, k_v), (v_hbm, v_v), (lam_hbm, lam_s)]
        )
    ]
    for c in loads:
        c.start()

    barrier = pltpu.get_barrier_semaphore()

    def tell(c, h):
        pl.semaphore_signal(barrier, inc=1, device_id=(c, h), device_id_type=MESH)

    heads = range(NH)
    for s in (1, 2):

        @pl.when(behind(s))
        def _():
            for d in heads:
                tell(ctx(-s), head(d))

        @pl.when(ahead(s))
        def _():
            for d in heads:
                tell(ctx(s), head(d))

        @pl.when(~behind(s))
        def _():
            for d in heads:
                tell(me - s + PLANE, head(d))

    for d in range(1, PLANE):
        tell(z * PLANE + lax.rem(r8 + d, PLANE), hd)
    for d in range(1, NH):
        tell(me, head(d))

    @pl.when(z < EARLY)
    def _():
        for d in range(1, DEPTH):
            tell(line(d), hd)

    @pl.when(host)
    def _():
        for d in range(1, NH):
            tell(guest, head(d))

    def when(condition, count):
        return jnp.where(condition, count, 0)

    pl.semaphore_wait(
        barrier,
        sum(when(ahead(s), NH) + when(behind(s), NH) + when(hosts(s), NH) for s in (1, 2))
        + EARLY - when(z < EARLY, 1) + when(last_two, NH - 1) + (NH - 1) + (PLANE - 1),
    )

    @pl.when(z > 0)
    def _():
        pl.semaphore_signal(line_sem.at[0], inc=1, device_id=(r8, hd), device_id_type=MESH)

    @pl.when(last_two)
    def _():
        for d in heads:
            pl.semaphore_signal(line_sem.at[2], inc=1, device_id=(r8, head(d)), device_id_type=MESH)

    def map_cols(g, m):
        return pl.ds(g * W + m * 128, 128)

    def send_first(g, s):
        for i, (ref, cols, lanes) in enumerate(
            ((q_v, map_cols(g, 1), pl.ds(0, 128)), (do_v, pl.ds(g * W, W), pl.ds(128, W)))
        ):
            pltpu.make_async_remote_copy(
                src_ref=ref.at[1, :, cols], dst_ref=r_a.at[g, s - 1, :, lanes],
                send_sem=qs_send.at[s - 1, i], recv_sem=a_recv.at[s - 1, g],
                device_id=(ctx(s), hd), device_id_type=MESH,
            ).start()

    def send_second(g, s):
        pltpu.make_async_remote_copy(
            src_ref=q_v.at[1, :, map_cols(g, 0)], dst_ref=r_b.at[g, s - 1],
            send_sem=qs_send.at[s - 1, 2], recv_sem=b_recv.at[s - 1, g],
            device_id=(ctx(s), hd), device_id_type=MESH,
        ).start()

    def send_nd(dst, c, send, recv):
        pltpu.make_async_remote_copy(
            src_ref=nd, dst_ref=dst, send_sem=send, recv_sem=recv, device_id=(c, hd), device_id_type=MESH
        ).start()

    for c in loads:
        c.wait()
    for half in range(2):
        lanes = pl.ds(half * BLK, BLK)
        for i in range(HG):
            nd[2 * i : 2 * i + 2, lanes] = nv[half, i]
            nd[8 + 2 * i : 10 + 2 * i, lanes] = dv_[half, i]

    @pl.when(last_two)
    def _():
        send_nd(h_nd, r8, hs_send.at[2], hn_recv)
        for g in range(HG):
            for i, ref in enumerate((q_v, do_v)):
                pltpu.make_async_remote_copy(
                    src_ref=ref.at[:, :, pl.ds(g * W, W)], dst_ref=h_qd.at[g, :, :, pl.ds(i * W, W)],
                    send_sem=hs_send.at[i], recv_sem=h_recv.at[g],
                    device_id=(r8, hd), device_id_type=MESH,
                ).start()

    for s in (1, 2):

        @pl.when(ahead(s))
        def _():
            send_nd(rnd.at[s - 1], ctx(s), nd_send.at[s - 1], nd_recv.at[s - 1])

    odd = r8 % 2 == 1
    for g in range(HG):
        for s in (2, 1):

            @pl.when(ahead(s) & ~odd if g == 0 and s == 1 else ahead(s))
            def _():
                send_first(g, s)

    for s in (1, 2):

        @pl.when(~behind(s))
        def _():
            for g in range(HG):
                for i, ref in enumerate((k_v, v_v)):
                    pltpu.make_async_remote_copy(
                        src_ref=ref.at[0, :, pl.ds(g * W, W)], dst_ref=w_kv.at[g, s - 1, :, pl.ds(i * W, W)],
                        send_sem=ws_send.at[s - 1, i], recv_sem=w_recv.at[s - 1, g],
                        device_id=(me - s + PLANE, hd), device_id_type=MESH,
                    ).start()


    for s in (1, 2):

        @pl.when(~behind(s))
        def _():
            r_a[:, s - 1] = jnp.zeros((HG, BLK, 128 + W), BF16)
            r_b[:, s - 1] = jnp.zeros((HG, BLK, 128), BF16)
            rnd[s - 1] = jnp.zeros((16, 128), F32)

    @pl.when(me == PLANE - 2)
    def _():
        w_kv[:, 0] = jnp.zeros((HG, BLK, 2 * W), BF16)

    @pl.when(me == n - 1)
    def _():
        back[0] = jnp.zeros((ROWS, COLS), BF16)

    kk = lax.broadcasted_iota(jnp.int32, (128, 128), 0)
    qq = lax.broadcasted_iota(jnp.int32, (128, 128), 1)
    own_mask = ((kk < 64) & (qq >= 64)) | (((kk < 64) == (qq < 64)) & (kk <= qq))
    rem_mask = (kk < 64) | (qq < 64) | (me >= 2)
    rem_mask = rem_mask & (me >= jnp.where(qq < 64, 1, 2))
    wrap_mask = (kk >= 64) | (me == PLANE - 1)

    def rows_of(ref, g):
        return [ref[i : i + 1, :] for i in (2 * g, 2 * g + 1, 8 + 2 * g, 9 + 2 * g)]

    def own(ref, g):
        return ref[:, :, pl.ds(g * W, W)].reshape(2 * BLK, W)

    def own_map(ref, g, m):
        return ref[:, :, map_cols(g, m)].reshape(2 * BLK, 128)

    def first(ref, g):
        both = ref[g].reshape(2 * BLK, 128 + W)
        return both[:, :128], both[:, 128:]

    def second(ref, g):
        return ref[g].reshape(2 * BLK, 128)

    def pair(ref, g):
        both = ref[g].reshape(2 * BLK, 2 * W)
        return both[:, :128], both[:, 128:W], both[:, W:]

    def out_cols(g):
        return pl.ds(pl.multiple_of((hd * HG + g) * W, W), W)

    def rows_at(h):
        return pl.ds(pl.multiple_of(h * ROWS, ROWS), ROWS)

    def spread(g):
        for d in range(1, NH):
            pltpu.make_async_remote_copy(
                src_ref=stage.at[g, :, rows_at(head(d)), :], dst_ref=landed.at[:, :, out_cols(g)],
                send_sem=r_send.at[g], recv_sem=r_recv,
                device_id=(me, head(d)), device_id_type=MESH,
            ).start()
        pltpu.make_async_copy(
            stage.at[g, :, rows_at(hd), :], landed.at[:, :, out_cols(g)], own_sem
        ).start()
        pass

    lam_tile[...] = jnp.zeros((8, 128), F32)
    for g in range(HG):
        q0, q1, do = own_map(q_v, g, 0), own_map(q_v, g, 1), own(do_v, g)
        k0, k1, v = own_map(k_v, g, 0), own_map(k_v, g, 1), own(v_v, g)
        p1, inner, lam_row = second_map(q1, do, k1, v, rows_of(nd, g), own_mask)
        dq, dk, dv = gradients(p1, inner, q0, q1, do, k0, k1, rows_of(nd, g), lam_s[g], own_mask)
        stage[g, 0:2] = rounded(dq)
        acc[g, 0] = dk
        acc[g, 1] = dv
        lam_tile[g : g + 1, :] = lam_row

    sent = [q_v.at[0, :, pl.ds(0, c)] for c in (HG * 128, HG * W, (HG - 1) * 128, (HG - 1) * W)]
    relays = odd & behind(2)

    @pl.when(relays)
    def _():
        wait_for(r_a.at[0, 1], a_recv.at[1, 0])
        pltpu.make_async_remote_copy(
            src_ref=r_a.at[0, 1], dst_ref=r_a.at[0, 0], send_sem=f_send, recv_sem=a_recv.at[0, 0],
            device_id=(ctx(-1), hd), device_id_type=MESH,
        ).start()

    for s in (1, 2):

        @pl.when(ahead(s) & ~odd if s == 1 else ahead(s))
        def _():
            wait_for(sent[0], qs_send.at[s - 1, 0])
            wait_for(sent[1], qs_send.at[s - 1, 1])

        if s == 1:

            @pl.when(ahead(s) & odd)
            def _():
                wait_for(sent[2], qs_send.at[0, 0])
                wait_for(sent[3], qs_send.at[0, 1])

        @pl.when(ahead(s))
        def _():
            for g in range(HG):
                send_second(g, s)


    for s in (1, 2):

        @pl.when(behind(s))
        def _():
            wait_for(rnd.at[s - 1], nd_recv.at[s - 1])

    left = lax.broadcasted_iota(jnp.int32, (16, 128), 1) < BLK
    ndr[...] = jnp.where(left, pltpu.roll(rnd[0], BLK, 1), rnd[1])

    for g in range(HG):
        for s in (1, 2):

            @pl.when(behind(s) & ~relays if g == 0 and s == 2 else behind(s))
            def _():
                wait_for(r_a.at[g, s - 1], a_recv.at[s - 1, g])

        q1, do = first(r_a, g)
        r_p1[g], r_in[g], lam_row = second_map(q1, do, own_map(k_v, g, 1), own(v_v, g), rows_of(ndr, g), rem_mask)
        lam_tile[g : g + 1, :] += lam_row

    def sum_over_plane():
        lbuf1[r8] = lam_tile[...]
        for d in range(1, PLANE):
            pltpu.make_async_remote_copy(
                src_ref=lbuf1.at[r8], dst_ref=lbuf1.at[r8],
                send_sem=l_send.at[0], recv_sem=l_recv.at[0],
                device_id=(z * PLANE + lax.rem(r8 + d, PLANE), hd), device_id_type=MESH,
            ).start()
        pass

    def sum_over_line():
        wait_for(lbuf1.at[pl.ds(0, PLANE - 1)], l_recv.at[0])
        total = lbuf1[0]
        for i in range(1, PLANE):
            total = total + lbuf1[i]
        lbuf2[z] = total

        def send_sum(to):
            @pl.when(z != to)
            def _():
                pltpu.make_async_remote_copy(
                    src_ref=lbuf2.at[z], dst_ref=lbuf2.at[z],
                    send_sem=l_send.at[1], recv_sem=l_recv.at[1],
                    device_id=(to * PLANE + r8, hd), device_id_type=MESH,
                ).start()

        for to in range(EARLY):
            send_sum(to)

        @pl.when(z > 0)
        def _():
            pl.semaphore_wait(line_sem.at[1], 1)

        for to in range(EARLY, DEPTH):
            send_sum(to)

    @pl.when(z > 0)
    def _():
        sum_over_plane()

    for g in range(HG):
        for s in (1, 2):

            @pl.when(behind(s))
            def _():
                wait_for(r_b.at[g, s - 1], b_recv.at[s - 1, g])

        q1, do = first(r_a, g)
        dq, dk, dv = gradients(
            r_p1[g], r_in[g], second(r_b, g), q1, do, own_map(k_v, g, 0), own_map(k_v, g, 1),
            rows_of(ndr, g), lam_s[g], rem_mask,
        )
        for s in (1, 2):
            st_p[s - 1, :, pl.ds(g * W, W)] = rounded(dq)[s - 1]
        stage[g, 2:4] = rounded(acc[g, 0] + dk)
        stage[g, 4:6] = rounded(acc[g, 1] + dv)
        spread(g)
        if g == 1:

            @pl.when(z > 0)
            def _():
                sum_over_line()

    all_cols = pl.ds(pl.multiple_of(hd * HG * W, W), HG * W)
    for s in (1, 2):

        @pl.when(behind(s))
        def _():
            for d in heads:
                pltpu.make_async_remote_copy(
                    src_ref=st_p.at[s - 1, rows_at(head(d)), :], dst_ref=back.at[s - 1, :, all_cols],
                    send_sem=p_send.at[s - 1], recv_sem=p_recv.at[s - 1],
                    device_id=(ctx(-s), head(d)), device_id_type=MESH,
                ).start()


    @pl.when(host)
    def _():
        pl.semaphore_wait(line_sem.at[2], NH)
        wait_for(h_nd, hn_recv)
        for g in range(HG):
            for s in (1, 2):

                @pl.when(hosts(s))
                def _():
                    wait_for(w_kv.at[g, s - 1], w_recv.at[s - 1, g])

            wait_for(h_qd.at[g], h_recv.at[g])
            q0, q1, do = pair(h_qd, g)
            k0, k1, v = pair(w_kv, g)
            p1, inner, lam_row = second_map(q1, do, k1, v, rows_of(h_nd, g), wrap_mask)
            lam_tile[g : g + 1, :] += lam_row
            dq, dk, dv = gradients(p1, inner, q0, q1, do, k0, k1, rows_of(h_nd, g), lam_s[g], wrap_mask)
            st_wq[g] = rounded(dq)
            for s in (1, 2):
                st_wkv[g, s - 1, 0] = rounded(dk)[s - 1]
                st_wkv[g, s - 1, 1] = rounded(dv)[s - 1]
            for s in (1, 2):

                @pl.when(hosts(s))
                def _():
                    for d in heads:
                        pltpu.make_async_remote_copy(
                            src_ref=st_wkv.at[g, s - 1, :, rows_at(head(d)), :],
                            dst_ref=wkv.at[s - 1, :, :, out_cols(g)],
                            send_sem=pw_send.at[s - 1, g], recv_sem=pw_recv.at[s - 1],
                            device_id=(me + s - PLANE, head(d)), device_id_type=MESH,
                        ).start()

            for d in heads:
                pltpu.make_async_remote_copy(
                    src_ref=st_wq.at[g, :, rows_at(head(d)), :], dst_ref=wq.at[:, :, out_cols(g)],
                    send_sem=wq_send.at[g], recv_sem=wq_recv,
                    device_id=(guest, head(d)), device_id_type=MESH,
                ).start()

    @pl.when(z == 0)
    def _():
        sum_over_plane()

    @pl.when(z == 0)
    def _():
        pl.semaphore_wait(line_sem.at[0], DEPTH - 1)
        for d in range(1, DEPTH):
            pl.semaphore_signal(line_sem.at[1], inc=1, device_id=(line(d), hd), device_id_type=MESH)

    @pl.when(z == 0)
    def _():
        sum_over_line()

    wait_for(landed.at[:, :, pl.ds(0, (NH - 1) * HG * W)], r_recv)
    for g in range(HG):
        wait_for(stage.at[g, :, pl.ds(0, ROWS)], own_sem)
    for s in (1, 2):

        @pl.when(ahead(s))
        def _():
            wait_for(back.at[s - 1], p_recv.at[s - 1])

        @pl.when(~behind(s))
        def _():
            wait_for(wkv.at[s - 1], pw_recv.at[s - 1])

    @pl.when(me < 2)
    def _():
        for i in range(2):
            first_term = jnp.where(me == 0, wkv[0, i].astype(F32), 0.0)
            total = landed[2 + 2 * i].astype(F32) + first_term + wkv[1, i].astype(F32)
            landed[2 + 2 * i] = total.astype(BF16)

    @pl.when(last_two)
    def _():
        wait_for(wq, wq_recv)
        landed[0] = (landed[0].astype(F32) + wq[0].astype(F32)).astype(BF16)
        back[1] = wq[1]


    for s in (1, 2):

        @pl.when(ahead(s))
        def _():
            wait_for(sent[0], qs_send.at[s - 1, 2])
            wait_for(nd, nd_send.at[s - 1])
            pass

        @pl.when(~behind(s))
        def _():
            wait_for(sent[1], ws_send.at[s - 1, 0])
            wait_for(sent[1], ws_send.at[s - 1, 1])
            pass

        @pl.when(behind(s))
        def _():
            wait_for(st_p.at[s - 1], p_send.at[s - 1])

        @pl.when(hosts(s))
        def _():
            for g in range(HG):
                wait_for(st_wkv.at[g, s - 1], pw_send.at[s - 1, g])


    @pl.when(relays)
    def _():
        wait_for(r_a.at[0, 1], f_send)

    @pl.when(host)
    def _():
        for g in range(HG):
            wait_for(st_wq.at[g], wq_send.at[g])
        pass

    @pl.when(last_two)
    def _():
        wait_for(q_v, hs_send.at[0])
        wait_for(q_v, hs_send.at[1])
        wait_for(nd, hs_send.at[2])
        pass

    for g in range(HG):
        wait_for(stage.at[g, :, pl.ds(0, (NH - 1) * ROWS)], r_send.at[g])
    wait_for(lbuf1.at[pl.ds(0, PLANE - 1)], l_send.at[0])
    wait_for(lbuf2.at[pl.ds(0, DEPTH - 1)], l_recv.at[1])
    wait_for(lbuf2.at[pl.ds(0, DEPTH - 1)], l_send.at[1])


def finish_kernel(landed, back, lbuf2, oq, ok, ov, lam_out, sum_q, sems):
    copies = [
        pltpu.make_async_copy(landed.at[pl.ds(2, 2)], ok, sems.at[0]),
        pltpu.make_async_copy(landed.at[pl.ds(4, 2)], ov, sems.at[1]),
        pltpu.make_async_copy(landed.at[0], oq.at[0], sems.at[2]),
        pltpu.make_async_copy(sum_q, oq.at[1], sems.at[3]),
    ]
    for c in copies[:3]:
        c.start()
    sum_q[...] = (landed[1].astype(F32) + back[0].astype(F32) + back[1].astype(F32)).astype(BF16)
    copies[3].start()
    total = lbuf2[0]
    for i in range(1, DEPTH):
        total = total + lbuf2[i]
    for g in range(HG):
        lam_out[g] = -jnp.sum(total[g : g + 1, :])
    for c in copies:
        c.wait()


def local(query_rows, key_rows, value_rows, out_grad, log_norms, row_deltas, lambdas):
    n = lax.axis_size("ctx")
    hbm = pl.BlockSpec(memory_space=pl.ANY)
    vmem = pl.BlockSpec(memory_space=pltpu.VMEM)
    smem = pl.BlockSpec(memory_space=pltpu.SMEM)
    half = (2, BLK, HG * W)
    dma, regular = pltpu.SemaphoreType.DMA, pltpu.SemaphoreType.REGULAR
    args = (
        query_rows, key_rows, value_rows, out_grad,
        jnp.swapaxes(log_norms, 1, 2), jnp.swapaxes(row_deltas, 1, 2), lambdas,
    )
    landed, back, sums = pl.pallas_call(
        functools.partial(main_kernel, n),
        out_shape=(
            pltpu.VMEM((6, ROWS, COLS), BF16), pltpu.VMEM((2, ROWS, COLS), BF16),
            pltpu.VMEM((DEPTH, 8, 128), F32),
        ),
        in_specs=[hbm] * 7,
        out_specs=(vmem,) * 3,
        scratch_shapes=[
            pltpu.SMEM((HG,), F32),
            pltpu.VMEM(half, BF16), pltpu.VMEM(half, BF16), pltpu.VMEM(half, BF16), pltpu.VMEM(half, BF16),
            pltpu.VMEM((2, HG, 2, BLK), F32), pltpu.VMEM((2, HG, 2, BLK), F32),
            pltpu.VMEM((16, 128), F32), pltpu.VMEM((16, 128), F32), pltpu.VMEM((2, 16, 128), F32),
            *[pltpu.VMEM((HG, 2, BLK, c), BF16) for c in (128 + W, 128, 2 * W, 2 * W)],
            pltpu.VMEM((16, 128), F32),
            *[pltpu.VMEM((HG, 2 * BLK, 2 * BLK), F32) for _ in range(2)],
            pltpu.VMEM((HG, 2, 2 * BLK, W), F32), pltpu.VMEM((HG, 6, BLK, W), BF16),
            pltpu.VMEM((2, BLK, HG * W), BF16),
            pltpu.VMEM((HG, 2, 2, BLK, W), BF16), pltpu.VMEM((HG, 2, BLK, W), BF16),
            pltpu.VMEM((2, 2, ROWS, COLS), BF16), pltpu.VMEM((2, ROWS, COLS), BF16),
            pltpu.VMEM((8, 128), F32), pltpu.VMEM((PLANE, 8, 128), F32),
            dma((7,)), dma, dma((2, 3)), dma((2, HG)), dma((2, HG)), dma, dma((2,)), dma((2,)),
            dma((2, 2)), dma((2, HG)), dma((3,)), dma((HG,)), dma, dma((HG,)), dma,
            dma((HG,)), dma, dma((2,)), dma((2,)), dma((2, HG)), dma((2,)), dma((2,)), dma((2,)),
            regular((3,)),
        ],
        compiler_params=pltpu.CompilerParams(
            collective_id=0, has_side_effects=True, vmem_limit_bytes=24 * 1024 * 1024
        ),
        cost_estimate=pl.CostEstimate(flops=3 * 10**8, bytes_accessed=2 * 10**6, transcendentals=2 * 10**5),
        name="attention_backward",
    )(*[pltpu.with_memory_space_constraint(x, pltpu.HBM) for x in args])
    out = jax.ShapeDtypeStruct((2, ROWS, COLS), BF16)
    return pl.pallas_call(
        finish_kernel,
        out_shape=(out, out, out, jax.ShapeDtypeStruct((HG,), F32)),
        in_specs=[vmem] * 3,
        out_specs=(hbm, hbm, hbm, smem),
        scratch_shapes=[pltpu.VMEM((ROWS, COLS), BF16), dma((4,))],
        compiler_params=pltpu.CompilerParams(vmem_limit_bytes=16 * 1024 * 1024),
        name="write_outputs",
    )(*[pltpu.with_memory_space_constraint(x, pltpu.VMEM) for x in (landed, back, sums)])


def solution(mesh):
    in_specs = (
        P(None, "ctx", "head"),
        P(None, "ctx", "head"),
        P(None, "ctx", "head"),
        P(None, "ctx", "head"),
        P(None, None, "head", "ctx"),
        P(None, None, "head", "ctx"),
        P("head"),
    )
    out_specs = (
        P(None, ("ctx", "head"), None),
        P(None, ("ctx", "head"), None),
        P(None, ("ctx", "head"), None),
        P("head"),
    )
    return jax.shard_map(local, mesh=mesh, in_specs=in_specs, out_specs=out_specs, check_vma=False)
```

time: 39.5 us -> 36.9 us (0.934)
  Pallas kernels: 38.5 us -> 35.9 us
    pallas_call x1, Pallas kernels: 37.2 us -> 34.5 us  [local(): pl.pallas_call(functools.partial(main_kernel, n), out_shape=(pltpu.VMEM((...]
where the time goes in v4:
time: 36.9 us; the launch traced here: 36.5 us
  Pallas kernels  35.9 us (97%)
  between operations  0.64 us (2%)
    pallas_call x1, Pallas kernels, local(): pl.pallas_call(functools.partial(main_kernel, n), out_shape=(pltpu.VMEM((...  34.5 us
    pallas_call x1, Pallas kernels, local(): pl.pallas_call(finish_kernel, out_shape=(out, out, out, jax.ShapeDtypeStr...  1.36 us

profile of v4, /device:TPU:6, one launch (start us, length us, event | category | flops | bytes accessed | tf_op | source)
XLA Modules:
  0.0 36.5 jit_solution(15498830397601685057)
XLA Ops:
  0.6 34.5 %attention_backward.1 = (bf16[6,16,3072]{2,1,0:T(8,128)(2,1)S(1)}, bf16[2,16,3072]{2,1,0:T(8,128)(2,1)S(1)}, f32[16,8,128]{2,1,0:T(8,128)S(1)}) custom-call(bf16[2,64,768]{2,1,0:T(8,128)(2,1)} %q_hbm.1, bf16[2,64,768]{2,1,0:T(8,128)(2,1)} %k_hbm.1, bf16[2,64,768]{2,1,0:T(8,128)(2,1)} %v_hbm.1, bf16[2,64,768]{2,1,0:T(8,128)(2,1)} %do_hbm.1, ...), custom_call_target="tpu_custom_call" | custom-call | flops 300000000 | bytes 2000000 | tf_op jit(solution)/shard_map/attention_backward/pallas_call | solution.py:594
  35.2 1.4 %write_outputs.1 = (bf16[2,16,3072]{2,1,0:T(8,128)(2,1)}, bf16[2,16,3072]{2,1,0:T(8,128)(2,1)}, bf16[2,16,3072]{2,1,0:T(8,128)(2,1)}, f32[3]{0:T(128)}) custom-call(bf16[6,16,3072]{2,1,0:T(8,128)(2,1)S(1)} %get-tuple-element.7.landed, bf16[2,16,3072]{2,1,0:T(8,128)(2,1)S(1)} %get-tuple-element.8.back, f32[16,8,128]{2,1,0:T(8,128)S(1)} %get-tuple-element.9.lbuf2), custom_call_target="tpu_custom_call" | custom-call | tf_op jit(solution)/shard_map/write_outputs/pallas_call | solution.py:627

commit v5 on v4

--- a/solution.py
+++ b/solution.py
@@ -146,6 +146,14 @@
     def when(condition, count):
         return jnp.where(condition, count, 0)
 
+    for c in loads:
+        c.wait()
+    for half in range(2):
+        lanes = pl.ds(half * BLK, BLK)
+        for i in range(HG):
+            nd[2 * i : 2 * i + 2, lanes] = nv[half, i]
+            nd[8 + 2 * i : 10 + 2 * i, lanes] = dv_[half, i]
+
     pl.semaphore_wait(
         barrier,
         sum(when(ahead(s), NH) + when(behind(s), NH) + when(hosts(s), NH) for s in (1, 2))
@@ -185,14 +193,6 @@
         pltpu.make_async_remote_copy(
             src_ref=nd, dst_ref=dst, send_sem=send, recv_sem=recv, device_id=(c, hd), device_id_type=MESH
         ).start()
-
-    for c in loads:
-        c.wait()
-    for half in range(2):
-        lanes = pl.ds(half * BLK, BLK)
-        for i in range(HG):
-            nd[2 * i : 2 * i + 2, lanes] = nv[half, i]
-            nd[8 + 2 * i : 10 + 2 * i, lanes] = dv_[half, i]
 
     @pl.when(last_two)
     def _():
@@ -315,24 +315,29 @@
             device_id=(ctx(-1), hd), device_id_type=MESH,
         ).start()
 
-    for s in (1, 2):
-
-        @pl.when(ahead(s) & ~odd if s == 1 else ahead(s))
-        def _():
-            wait_for(sent[0], qs_send.at[s - 1, 0])
-            wait_for(sent[1], qs_send.at[s - 1, 1])
-
-        if s == 1:
-
-            @pl.when(ahead(s) & odd)
+    def send_rest():
+        for s in (1, 2):
+
+            @pl.when(ahead(s) & ~odd if s == 1 else ahead(s))
             def _():
-                wait_for(sent[2], qs_send.at[0, 0])
-                wait_for(sent[3], qs_send.at[0, 1])
-
-        @pl.when(ahead(s))
-        def _():
-            for g in range(HG):
-                send_second(g, s)
+                wait_for(sent[0], qs_send.at[s - 1, 0])
+                wait_for(sent[1], qs_send.at[s - 1, 1])
+
+            if s == 1:
+
+                @pl.when(ahead(s) & odd)
+                def _():
+                    wait_for(sent[2], qs_send.at[0, 0])
+                    wait_for(sent[3], qs_send.at[0, 1])
+
+            @pl.when(ahead(s))
+            def _():
+                for g in range(HG):
+                    send_second(g, s)
+
+    @pl.when(z == 0)
+    def _():
+        send_rest()
 
 
     for s in (1, 2):
@@ -365,35 +370,31 @@
             ).start()
         pass
 
+    def send_sum(to):
+        @pl.when(z != to)
+        def _():
+            pltpu.make_async_remote_copy(
+                src_ref=lbuf2.at[z], dst_ref=lbuf2.at[z],
+                send_sem=l_send.at[1], recv_sem=l_recv.at[1],
+                device_id=(to * PLANE + r8, hd), device_id_type=MESH,
+            ).start()
+
+        pass
+
     def sum_over_line():
         wait_for(lbuf1.at[pl.ds(0, PLANE - 1)], l_recv.at[0])
         total = lbuf1[0]
         for i in range(1, PLANE):
             total = total + lbuf1[i]
         lbuf2[z] = total
-
-        def send_sum(to):
-            @pl.when(z != to)
-            def _():
-                pltpu.make_async_remote_copy(
-                    src_ref=lbuf2.at[z], dst_ref=lbuf2.at[z],
-                    send_sem=l_send.at[1], recv_sem=l_recv.at[1],
-                    device_id=(to * PLANE + r8, hd), device_id_type=MESH,
-                ).start()
-
         for to in range(EARLY):
             send_sum(to)
 
-        @pl.when(z > 0)
-        def _():
-            pl.semaphore_wait(line_sem.at[1], 1)
-
-        for to in range(EARLY, DEPTH):
-            send_sum(to)
-
     @pl.when(z > 0)
     def _():
         sum_over_plane()
+        send_rest()
+        sum_over_line()
 
     for g in range(HG):
         for s in (1, 2):
@@ -412,12 +413,6 @@
         stage[g, 2:4] = rounded(acc[g, 0] + dk)
         stage[g, 4:6] = rounded(acc[g, 1] + dv)
         spread(g)
-        if g == 1:
-
-            @pl.when(z > 0)
-            def _():
-                sum_over_line()
-
     all_cols = pl.ds(pl.multiple_of(hd * HG * W, W), HG * W)
     for s in (1, 2):
 
@@ -484,6 +479,13 @@
     @pl.when(z == 0)
     def _():
         sum_over_line()
+
+    @pl.when(z > 0)
+    def _():
+        pl.semaphore_wait(line_sem.at[1], 1)
+
+    for to in range(EARLY, DEPTH):
+        send_sum(to)
 
     wait_for(landed.at[:, :, pl.ds(0, (NH - 1) * HG * W)], r_recv)
     for g in range(HG):

time: 36.9 us -> 37.1 us (level)
  no operation moved by 1% of the time
where the time goes in v5:
time: 37.1 us; the launch traced here: 36.6 us
  Pallas kernels  35.9 us (97%)
  between operations  0.64 us (2%)
    pallas_call x1, Pallas kernels, local(): pl.pallas_call(functools.partial(main_kernel, n), out_shape=(pltpu.VMEM((...  34.6 us
    pallas_call x1, Pallas kernels, local(): pl.pallas_call(finish_kernel, out_shape=(out, out, out, jax.ShapeDtypeStr...  1.36 us

profile of v5, /device:TPU:6, one launch (start us, length us, event | category | flops | bytes accessed | tf_op | source)
XLA Modules:
  0.0 36.6 jit_solution(17196626448712728836)
XLA Ops:
  0.6 34.6 %attention_backward.1 = (bf16[6,16,3072]{2,1,0:T(8,128)(2,1)S(1)}, bf16[2,16,3072]{2,1,0:T(8,128)(2,1)S(1)}, f32[16,8,128]{2,1,0:T(8,128)S(1)}) custom-call(bf16[2,64,768]{2,1,0:T(8,128)(2,1)} %q_hbm.1, bf16[2,64,768]{2,1,0:T(8,128)(2,1)} %k_hbm.1, bf16[2,64,768]{2,1,0:T(8,128)(2,1)} %v_hbm.1, bf16[2,64,768]{2,1,0:T(8,128)(2,1)} %do_hbm.1, ...), custom_call_target="tpu_custom_call" | custom-call | flops 300000000 | bytes 2000000 | tf_op jit(solution)/shard_map/attention_backward/pallas_call | solution.py:596
  35.2 1.4 %write_outputs.1 = (bf16[2,16,3072]{2,1,0:T(8,128)(2,1)}, bf16[2,16,3072]{2,1,0:T(8,128)(2,1)}, bf16[2,16,3072]{2,1,0:T(8,128)(2,1)}, f32[3]{0:T(128)}) custom-call(bf16[6,16,3072]{2,1,0:T(8,128)(2,1)S(1)} %get-tuple-element.7.landed, bf16[2,16,3072]{2,1,0:T(8,128)(2,1)S(1)} %get-tuple-element.8.back, f32[16,8,128]{2,1,0:T(8,128)S(1)} %get-tuple-element.9.lbuf2), custom_call_target="tpu_custom_call" | custom-call | tf_op jit(solution)/shard_map/write_outputs/pallas_call | solution.py:629

commit v6 on v4

--- a/solution.py
+++ b/solution.py
@@ -560,12 +560,13 @@
     wait_for(lbuf2.at[pl.ds(0, DEPTH - 1)], l_send.at[1])
 
 
-def finish_kernel(landed, back, lbuf2, oq, ok, ov, lam_out, sum_q, sems):
+def finish_kernel(landed, back, lbuf2, oq, ok, ov, lam_out, sum_q, sums, sems):
     copies = [
         pltpu.make_async_copy(landed.at[pl.ds(2, 2)], ok, sems.at[0]),
         pltpu.make_async_copy(landed.at[pl.ds(4, 2)], ov, sems.at[1]),
         pltpu.make_async_copy(landed.at[0], oq.at[0], sems.at[2]),
         pltpu.make_async_copy(sum_q, oq.at[1], sems.at[3]),
+        pltpu.make_async_copy(sums, lam_out, sems.at[4]),
     ]
     for c in copies[:3]:
         c.start()
@@ -575,7 +576,8 @@
     for i in range(1, DEPTH):
         total = total + lbuf2[i]
     for g in range(HG):
-        lam_out[g] = -jnp.sum(total[g : g + 1, :])
+        sums[g] = -jnp.sum(total[g : g + 1, :])
+    copies[4].start()
     for c in copies:
         c.wait()
 
@@ -584,7 +586,6 @@
     n = lax.axis_size("ctx")
     hbm = pl.BlockSpec(memory_space=pl.ANY)
     vmem = pl.BlockSpec(memory_space=pltpu.VMEM)
-    smem = pl.BlockSpec(memory_space=pltpu.SMEM)
     half = (2, BLK, HG * W)
     dma, regular = pltpu.SemaphoreType.DMA, pltpu.SemaphoreType.REGULAR
     args = (
@@ -628,8 +629,8 @@
         finish_kernel,
         out_shape=(out, out, out, jax.ShapeDtypeStruct((HG,), F32)),
         in_specs=[vmem] * 3,
-        out_specs=(hbm, hbm, hbm, smem),
-        scratch_shapes=[pltpu.VMEM((ROWS, COLS), BF16), dma((4,))],
+        out_specs=(hbm,) * 4,
+        scratch_shapes=[pltpu.VMEM((ROWS, COLS), BF16), pltpu.SMEM((HG,), F32), dma((5,))],
         compiler_params=pltpu.CompilerParams(vmem_limit_bytes=16 * 1024 * 1024),
         name="write_outputs",
     )(*[pltpu.with_memory_space_constraint(x, pltpu.VMEM) for x in (landed, back, sums)])

time: 36.9 us -> 36.4 us (0.986)
  Pallas kernels: 35.9 us -> 35.4 us
    pallas_call x1, Pallas kernels: 1.36 us -> 0.86 us  [local(): pl.pallas_call(finish_kernel, out_shape=(out, out, out, jax.ShapeDtypeStr...]
where the time goes in v6:
time: 36.4 us; the launch traced here: 36 us
  Pallas kernels  35.4 us (97%)
  between operations  0.64 us (2%)
    pallas_call x1, Pallas kernels, local(): pl.pallas_call(functools.partial(main_kernel, n), out_shape=(pltpu.VMEM((...  34.5 us
    pallas_call x1, Pallas kernels, local(): pl.pallas_call(finish_kernel, out_shape=(out, out, out, jax.ShapeDtypeStr...  0.86 us

profile of v6, /device:TPU:6, one launch (start us, length us, event | category | flops | bytes accessed | tf_op | source)
XLA Modules:
  0.0 36.0 jit_solution(3301450759845160457)
XLA Ops:
  0.6 34.5 %attention_backward.1 = (bf16[6,16,3072]{2,1,0:T(8,128)(2,1)S(1)}, bf16[2,16,3072]{2,1,0:T(8,128)(2,1)S(1)}, f32[16,8,128]{2,1,0:T(8,128)S(1)}) custom-call(bf16[2,64,768]{2,1,0:T(8,128)(2,1)} %q_hbm.1, bf16[2,64,768]{2,1,0:T(8,128)(2,1)} %k_hbm.1, bf16[2,64,768]{2,1,0:T(8,128)(2,1)} %v_hbm.1, bf16[2,64,768]{2,1,0:T(8,128)(2,1)} %do_hbm.1, ...), custom_call_target="tpu_custom_call" | custom-call | flops 300000000 | bytes 2000000 | tf_op jit(solution)/shard_map/attention_backward/pallas_call | solution.py:595
  35.2 0.9 %write_outputs.1 = (bf16[2,16,3072]{2,1,0:T(8,128)(2,1)}, bf16[2,16,3072]{2,1,0:T(8,128)(2,1)}, bf16[2,16,3072]{2,1,0:T(8,128)(2,1)}, f32[3]{0:T(128)}) custom-call(bf16[6,16,3072]{2,1,0:T(8,128)(2,1)S(1)} %get-tuple-element.7.landed, bf16[2,16,3072]{2,1,0:T(8,128)(2,1)S(1)} %get-tuple-element.8.back, f32[16,8,128]{2,1,0:T(8,128)S(1)} %get-tuple-element.9.lbuf2), custom_call_target="tpu_custom_call" | custom-call | tf_op jit(solution)/shard_map/write_outputs/pallas_call | solution.py:628

commit v7 on v6

--- a/solution.py
+++ b/solution.py
@@ -115,8 +115,7 @@
 
         @pl.when(behind(s))
         def _():
-            for d in heads:
-                tell(ctx(-s), head(d))
+            tell(ctx(-s), hd)
 
         @pl.when(ahead(s))
         def _():
@@ -148,7 +147,7 @@
 
     pl.semaphore_wait(
         barrier,
-        sum(when(ahead(s), NH) + when(behind(s), NH) + when(hosts(s), NH) for s in (1, 2))
+        sum(when(ahead(s), 1) + when(behind(s), NH) + when(hosts(s), NH) for s in (1, 2))
         + EARLY - when(z < EARLY, 1) + when(last_two, NH - 1) + (NH - 1) + (PLANE - 1),
     )
 

time: 36.4 us -> 36.7 us (level)
  Pallas kernels: 35.4 us -> 36 us
    pallas_call x1, Pallas kernels: 34.5 us -> 35.1 us  [local(): pl.pallas_call(functools.partial(main_kernel, n), out_shape=(pltpu.VMEM((...]
where the time goes in v7:
time: 36.7 us; the launch traced here: 36.6 us
  Pallas kernels  36 us (98%)
  between operations  0.64 us (2%)
    pallas_call x1, Pallas kernels, local(): pl.pallas_call(functools.partial(main_kernel, n), out_shape=(pltpu.VMEM((...  35.1 us
    pallas_call x1, Pallas kernels, local(): pl.pallas_call(finish_kernel, out_shape=(out, out, out, jax.ShapeDtypeStr...  0.86 us

profile of v7, /device:TPU:6, one launch (start us, length us, event | category | flops | bytes accessed | tf_op | source)
XLA Modules:
  0.0 36.6 jit_solution(7855225159569294243)
XLA Ops:
  0.6 35.1 %attention_backward.1 = (bf16[6,16,3072]{2,1,0:T(8,128)(2,1)S(1)}, bf16[2,16,3072]{2,1,0:T(8,128)(2,1)S(1)}, f32[16,8,128]{2,1,0:T(8,128)S(1)}) custom-call(bf16[2,64,768]{2,1,0:T(8,128)(2,1)} %q_hbm.1, bf16[2,64,768]{2,1,0:T(8,128)(2,1)} %k_hbm.1, bf16[2,64,768]{2,1,0:T(8,128)(2,1)} %v_hbm.1, bf16[2,64,768]{2,1,0:T(8,128)(2,1)} %do_hbm.1, ...), custom_call_target="tpu_custom_call" | custom-call | flops 300000000 | bytes 2000000 | tf_op jit(solution)/shard_map/attention_backward/pallas_call | solution.py:594
  35.7 0.9 %write_outputs.1 = (bf16[2,16,3072]{2,1,0:T(8,128)(2,1)}, bf16[2,16,3072]{2,1,0:T(8,128)(2,1)}, bf16[2,16,3072]{2,1,0:T(8,128)(2,1)}, f32[3]{0:T(128)}) custom-call(bf16[6,16,3072]{2,1,0:T(8,128)(2,1)S(1)} %get-tuple-element.7.landed, bf16[2,16,3072]{2,1,0:T(8,128)(2,1)S(1)} %get-tuple-element.8.back, f32[16,8,128]{2,1,0:T(8,128)S(1)} %get-tuple-element.9.lbuf2), custom_call_target="tpu_custom_call" | custom-call | tf_op jit(solution)/shard_map/write_outputs/pallas_call | solution.py:627
